TPU v7x, 32 devices: a whole 2x2x4 slice. The times are simulated.
32 devices in a mesh: seq: 16 (over z, y, x), head: 2 (over core).
Axes of the slice: x: 2, y: 2, z: 4, core: 2. Of those that a mesh axis runs over, the one named last changes fastest.
Arguments:
- layer_input: bfloat16 [2048, 4096], P('seq', 'head'), may hold values from -6 to 6
- query_rows: bfloat16 [2048, 2048], P('seq', 'head'), may hold values from -6 to 6
- key_matrix_rows: bfloat16 [2048, 2048], P('seq', 'head'), may hold values from -1.25 to 1.25
- value_rows: bfloat16 [2048, 2048], P('seq', 'head'), may hold values from -6 to 6
- beta_rows: float32 [2048, 16], P('seq', 'head'), may hold values from 0 to 0.9, as said below
- log_gate: float32 [2048, 16], P('seq', 'head'), may hold values from -1.3 to 0, as said below
- grad_out: bfloat16 [2048, 2048], P('seq', 'head'), may hold values from -6 to 6
Outputs:
- grad_query: bfloat16 [2048, 2048], P('seq', 'head')
- grad_key: bfloat16 [2048, 2048], P('seq', 'head')
- grad_value: bfloat16 [2048, 2048], P('seq', 'head')
- grad_beta: float32 [2048, 16], P('seq', 'head')
- grad_log_gate: float32 [2048, 16], P('seq', 'head')
- grad_weight: bfloat16 [4096, 2048], P(None, 'head')
Inputs may be any that keep to these rules, and one draw needn't show every extreme that they name: `beta_rows`: write strengths vary from token to token and from head to head. `log_gate`: decay rates vary from token to token and from head to head.
All inputs are finite; a program needn't handle non-finite values.
Results may differ from a plain program's by a relative error of at most 0.0049.
Values may be sent and summed in bfloat16 or wider, within the bound.
No kernel may reach another device: no remote copies, remote signals or barrier semaphores. Data moves between devices by JAX's collectives and lax.ppermute only.
A program may use at most 128 MiB of HBM per device.

v0:
```python
from functools import partial

import jax
import jax.numpy as jnp
from jax import lax
from jax.sharding import PartitionSpec as P

HD = 128
BLOCK = 64


HIGHEST_PRECISION = lax.Precision.HIGHEST


def carried_in(part, axis, combine, identity, reverse):
    count = lax.axis_size(axis)
    place = lax.axis_index(axis)
    ahead = count - 1 - place if reverse else place
    gathered = jax.tree.map(lambda a: lax.all_gather(a, axis), part)
    state = jax.tree.map(lambda a, e: jnp.zeros_like(a) + jnp.asarray(e, a.dtype), part, identity)

    def one(turn, state):
        source = count - 1 - turn if reverse else turn
        return combine(
            state, jax.tree.map(lambda a: lax.dynamic_index_in_dim(a, source, 0, False), gathered)
        )

    return lax.fori_loop(0, ahead, one, state)


def product(left_side, right_side):
    return jnp.matmul(left_side, right_side, precision=HIGHEST_PRECISION)


def flipped(matrix):
    return jnp.swapaxes(matrix, -1, -2)


def unit_inverse(strict_lower):
    order_size = strict_lower.shape[-1]
    identity = jnp.eye(order_size, dtype=strict_lower.dtype)
    result = identity - strict_lower
    exponent_summand = strict_lower
    covered = 2
    while covered < order_size:
        exponent_summand = product(exponent_summand, exponent_summand)
        result = product(result, identity + exponent_summand)
        covered = covered * 2
    return result


def block_parts(key_block, strength, log_decay):
    order_size = log_decay.shape[-1]
    running = jnp.cumsum(log_decay, axis=-1)
    line_number = lax.broadcasted_iota(jnp.int32, (order_size, order_size), 0)
    col_index = lax.broadcasted_iota(jnp.int32, (order_size, order_size), 1)
    causal = line_number >= col_index
    strict = line_number > col_index
    spread = running[..., :, None] - running[..., None, :]
    decay_table = jnp.where(causal, jnp.exp(jnp.where(causal, spread, 0.0)), 0.0)
    strict_lower = jnp.where(
        strict, strength[..., :, None] * decay_table * product(key_block, flipped(key_block)), 0.0
    )
    growth = jnp.exp(running)
    tail_decay = jnp.exp(running[..., -1:] - running)
    return (decay_table, growth, tail_decay, unit_inverse(strict_lower))


def segment(query_block, key_block, value_block, strength, log_decay, init_state, with_out):
    decay_table, growth, tail_decay, inverse = block_parts(key_block, strength, log_decay)
    pseudo = product(inverse, strength[..., None] * value_block)
    erasure = product(inverse, (strength * growth)[..., None] * key_block)
    written = flipped(tail_decay[..., None] * key_block)
    keep_all = growth[..., -1]
    argument_sequence = [pseudo, erasure, written, keep_all]
    if with_out:
        argument_sequence = argument_sequence + [
            decay_table * product(query_block, flipped(key_block)),
            growth[..., None] * query_block,
        ]

    def advance(carry_state, pieces):
        update = pieces[0] - product(pieces[1], carry_state)
        after_state = pieces[3] * carry_state + product(pieces[2], update)
        if with_out:
            return (after_state, product(pieces[5], carry_state) + product(pieces[4], update))
        return (after_state, None)

    return lax.scan(advance, init_state, tuple(argument_sequence))


def combine_maps(earlier, later):
    return (product(later[0], earlier[0]), product(later[0], earlier[1]) + later[1])


def shards(layer_input, query_rows, key_matrix_rows, value_rows, beta_rows, log_gate, grad_out):
    length = query_rows.shape[0]
    heads_here = beta_rows.shape[1]
    block_count = length // BLOCK

    def per_head_apply(matrix):
        return (
            matrix.reshape(block_count, BLOCK, heads_here, HD)
            .transpose(2, 0, 1, 3)
            .astype(jnp.float32)
        )

    def by_head_scalar(matrix):
        return matrix.reshape(block_count, BLOCK, heads_here).transpose(2, 0, 1)

    def to_rows(tensor):
        return tensor.transpose(1, 2, 0, 3).reshape(length, heads_here * HD).astype(jnp.bfloat16)

    queries = per_head_apply(query_rows)
    keys_local = per_head_apply(key_matrix_rows)
    values_local = per_head_apply(value_rows)
    grads_local = per_head_apply(grad_out)
    strength = by_head_scalar(beta_rows)
    decays = by_head_scalar(log_gate)
    run_states = jax.vmap(partial(segment, with_out=False))
    run_full = jax.vmap(partial(segment, with_out=True))
    identity = jnp.broadcast_to(jnp.eye(HD, dtype=jnp.float32), (heads_here, HD, HD))
    zero_state = jnp.zeros((heads_here, HD, HD), jnp.float32)
    stacked_start = jnp.concatenate([identity, zero_state], axis=2)
    widened = jnp.concatenate([jnp.zeros_like(values_local), values_local], axis=3)
    combined, unused = run_states(queries, keys_local, widened, strength, decays, stacked_start)
    transit = combined[:, :, :HD]
    offset = combined[:, :, HD:]

    def local_outputs(state_guess):
        return run_full(queries, keys_local, values_local, strength, decays, state_guess)[1]

    unused_out, pull_state = jax.vjp(local_outputs, zero_state)
    carried = pull_state(grads_local)[0]
    unused_map, entry_state = carried_in(
        (transit, offset), "seq", combine_maps, (identity, zero_state), False
    )
    unused_back, leaving = carried_in(
        (flipped(transit), carried), "seq", combine_maps, (identity, zero_state), True
    )

    def whole_layer(query_all, key_all, value_all, strength_all, decay_all):
        return run_full(query_all, key_all, value_all, strength_all, decay_all, entry_state)

    unused_pair, pull_back = jax.vjp(
        whole_layer, queries, keys_local, values_local, strength, decays
    )
    gradients = pull_back((leaving, grads_local))
    grad_value = to_rows(gradients[2])
    grad_beta = gradients[3].transpose(1, 2, 0).reshape(length, heads_here)
    grad_log_gate = gradients[4].transpose(1, 2, 0).reshape(length, heads_here)
    all_features = lax.all_gather(layer_input, "head", axis=1, tiled=True)
    own_rows = lax.psum_scatter(
        jnp.einsum("tc,th->ch", all_features, grad_value, preferred_element_type=jnp.float32),
        "seq",
        scatter_dimension=0,
        tiled=True,
    ).astype(jnp.bfloat16)
    grad_weight = lax.all_gather(own_rows, "seq", axis=0, tiled=True)
    return (
        to_rows(gradients[0]),
        to_rows(gradients[1]),
        grad_value,
        grad_beta,
        grad_log_gate,
        grad_weight,
    )


def solution(mesh):
    in_specs = (
        P("seq", "head"),
        P("seq", "head"),
        P("seq", "head"),
        P("seq", "head"),
        P("seq", "head"),
        P("seq", "head"),
        P("seq", "head"),
    )
    out_specs = (
        P("seq", "head"),
        P("seq", "head"),
        P("seq", "head"),
        P("seq", "head"),
        P("seq", "head"),
        P(None, "head"),
    )
    return jax.shard_map(shards, mesh=mesh, in_specs=in_specs, out_specs=out_specs, check_vma=False)
```

profile of v0, /device:TPU:0, one launch (start us, length us, event | category | flops | bytes accessed | tf_op | source)
XLA Modules:
  0.0 1086.4 jit_solution(13270316903014321868)
XLA Ops:
  19.5 2.4 fusion.130
  26.7 2.0 fusion.123
  30.7 2.1 convolution_bitcast_fusion.5
  36.4 7.6 while.103
  57.5 8.0 while.109
  61.5 2.0 convolution_add_fusion.35
  67.6 2.6 convolution_bitcast_fusion.10
  70.2 93.8 %all-gather.19.cloned.1.call-done = f32[128,128,128]{2,1,0:T(8,128)} async-done(((f32[8,128,128]{2,1,0:T(8,128)}), f32[128,128,128]{2,1,0:T(8,128)}) %all-gather.19.cloned.1.call-update) | async-done | bytes 8388624 | tf_op jit(solution)/shard_map/all_gather | solution.py:19
  163.9 113.8 %all-gather.21.cloned.1.call-done = f32[128,128,128]{2,1,0:T(8,128)} async-done(((f32[8,128,128]{2,1,0:T(8,128)}), f32[128,128,128]{2,1,0:T(8,128)}) %all-gather.21.cloned.1.call-update) | async-done | bytes 8388624 | tf_op jit(solution)/shard_map/all_gather | solution.py:19
  278.7 6.9 while.107
  278.7 2.2 bitcast_dynamic-update-slice_fusion.6
  282.1 2.3 bitcast_dynamic-update-slice_fusion.6
  285.6 106.0 %all-gather.17.cloned.1.call-done = f32[128,128,128]{2,1,0:T(8,128)} async-done(((f32[8,128,128]{2,1,0:T(8,128)}), f32[128,128,128]{2,1,0:T(8,128)}) %all-gather.17.cloned.1.call-update) | async-done | bytes 8388624 | tf_op jit(solution)/shard_map/all_gather | solution.py:19
  391.6 113.7 %all-gather.15.cloned.1.call-done = f32[128,128,128]{2,1,0:T(8,128)} async-done(((f32[8,128,128]{2,1,0:T(8,128)}), f32[128,128,128]{2,1,0:T(8,128)}) %all-gather.15.cloned.1.call-update) | async-done | bytes 8388624 | tf_op jit(solution)/shard_map/all_gather | solution.py:19
  505.3 29.4 %while.105 = (s32[]{:T(128)}, f32[8,128,128]{2,1,0:T(8,128)S(1)}, s32[]{:T(128)}, f32[16,8,128,128]{3,2,1,0:T(8,128)}, f32[16,8,128,128]{3,2,1,0:T(8,128)}, /*index=5*/s32[]{:T(128)}, s32[]{:T(128)}, s32[]{:T(128)}, s32[]{:T(128)}) while((s32[]{:T(128)}, f32[8,128,128]{2,1,0:T(8,128)S(1)}, s32[]{:T(128)}, f32[16,8,128,128]{3,2,1,0:T(8,128)}, ...), condition=%wide.region_8.9_spmd, body=%wide.region_7.8_spmd.sunk | while | flops 201457664 | bytes 3146891 | solution.py:28
  539.0 29.0 %while.108 = (s32[]{:T(128)}, f32[8,128,128]{2,1,0:T(8,128)S(1)}, f32[2,8,64,128]{3,2,1,0:T(8,128)}, f32[2,8,64,128]{3,2,1,0:T(8,128)}, f32[2,8,128,64]{2,3,0,1:...) while((s32[]{:T(128)}, f32[8,128,128]{2,1,0:T(8,128)S(1)}, ...), condition=%wide.region_15.16_spmd, body=%wide.region_13.15_spmd.sunk | while | flops 705495040 | bytes 10494817 | solution.py:89
  541.6 2.0 convolution_add_fusion.33
  543.8 2.8 fusion.353
  551.2 2.2 fusion.355
  558.2 2.8 fusion.353
  565.7 2.2 fusion.355
  568.0 3.1 multiply_reduce_fusion.1
  571.5 9.4 convolution_bitcast_fusion.4
  581.2 342.2 %reduce-scatter.2.cloned.1.call-done = f32[256,1024]{0,1:T(8,128)} async-done(((f32[4096,1024]{0,1:T(8,128)}), f32[256,1024]{0,1:T(8,128)}) %reduce-scatter.2.cloned.1.call-update) | async-done | bytes 1048592 | tf_op jit(solution)/shard_map/reduce_scatter | solution.py:153
  923.4 2.1 convert_element_type.100
  925.5 2.1 copy.276
  927.6 3.6 fusion.98
  935.0 2.1 fusion.96
  937.1 2.2 convolution_add_fusion.19
  958.7 2.3 fusion.104
  971.8 95.4 %all-gather.13.cloned.1.call-done = bf16[4096,1024]{0,1:T(8,128)(2,1)} async-done(((bf16[256,1024]{0,1:T(8,128)(2,1)}), bf16[4096,1024]{0,1:T(8,128)(2,1)}) %all-gather.13.cloned.1.call-update) | async-done | bytes 8388624 | tf_op jit(solution)/shard_map/all_gather | solution.py:159
  1067.1 11.9 %copy.280 = bf16[4096,1024]{1,0:T(8,128)(2,1)} copy(bf16[4096,1024]{0,1:T(8,128)(2,1)} %all-gather.13.cloned.1.call-done) | data formatting | bytes 16777216
  (308 shorter events, 139.6 us)
Async XLA Ops:
  7.2 156.8 %all-gather.19.cloned.1.call-start = ((), (), s32[]{:S(2)}) async-start(), calls=%async_computation.6 | async-start | bytes 8912896 | tf_op jit(solution)/shard_map/all_gather | solution.py:19
  10.5 13.7 %copy-start.14 = (f32[8,2,64,64]{2,3,1,0:T(8,128)}, f32[8,2,64,64]{2,3,1,0:T(8,128)S(1)}, u32[]{:S(2)}) copy-start(f32[8,2,64,64]{2,3,1,0:T(8,128)S(1)} %fusion.143) | copy-start | bytes 786436
  13.6 16.1 %copy-start.1 = (f32[8,2,64,64]{3,2,1,0:T(8,128)}, f32[8,2,64,64]{3,2,1,0:T(8,128)S(1)}, u32[]{:S(2)}) copy-start(f32[8,2,64,64]{3,2,1,0:T(8,128)S(1)} %fusion.200) | copy-start | bytes 786436
  13.8 14.9 %copy-start.20 = (f32[8,2,64,64]{2,3,1,0:T(8,128)}, f32[8,2,64,64]{2,3,1,0:T(8,128)S(1)}, u32[]{:S(2)}) copy-start(f32[8,2,64,64]{2,3,1,0:T(8,128)S(1)} %copy.194) | copy-start | bytes 786436
  14.4 18.3 %copy-start.3 = (f32[8,2,64,64]{3,2,1,0:T(8,128)}, f32[8,2,64,64]{3,2,1,0:T(8,128)S(1)}, u32[]{:S(2)}) copy-start(f32[8,2,64,64]{3,2,1,0:T(8,128)S(1)} %fusion.201) | copy-start | bytes 786436
  16.1 17.6 %copy-start.6 = (f32[8,2,64,64]{3,2,1,0:T(8,128)}, f32[8,2,64,64]{3,2,1,0:T(8,128)S(1)}, u32[]{:S(2)}) copy-start(f32[8,2,64,64]{3,2,1,0:T(8,128)S(1)} %fusion.202) | copy-start | bytes 786436
  18.5 10.2 copy-start.23
  18.5 15.3 %copy-start.47 = (f32[8,2]{0,1:T(2,128)S(1)}, f32[8,2]{0,1:T(2,128)}, u32[]{:S(2)}) copy-start(f32[8,2]{0,1:T(2,128)} %slice_reduce_fusion) | copy-start | bytes 196
  19.5 15.3 %copy-start.16 = (f32[8,2,64,64]{2,3,1,0:T(8,128)}, f32[8,2,64,64]{2,3,1,0:T(8,128)S(1)}, u32[]{:S(2)}) copy-start(f32[8,2,64,64]{2,3,1,0:T(8,128)S(1)} %convolution_add_fusion.20) | copy-start | bytes 786436
  30.7 36.9 %copy-start.8 = (f32[8,2,64,64]{3,2,1,0:T(8,128)}, f32[8,2,64,64]{3,2,1,0:T(8,128)S(1)}, u32[]{:S(2)}) copy-start(f32[8,2,64,64]{3,2,1,0:T(8,128)S(1)} %fusion.203) | copy-start | bytes 786436
  48.2 229.5 %all-gather.21.cloned.1.call-start = ((), (), s32[]{:S(2)}) async-start(), calls=%async_computation.7 | async-start | bytes 8912896 | tf_op jit(solution)/shard_map/all_gather | solution.py:19
  49.1 342.4 %all-gather.17.cloned.1.call-start = ((), (), s32[]{:S(2)}) async-start(), calls=%async_computation.5 | async-start | bytes 8912896 | tf_op jit(solution)/shard_map/all_gather | solution.py:19
  66.4 438.9 %all-gather.15.cloned.1.call-start = ((), (), s32[]{:S(2)}) async-start(), calls=%async_computation.4 | async-start | bytes 8912896 | tf_op jit(solution)/shard_map/all_gather | solution.py:19
  66.9 504.6 %all-gather.11.cloned.1.call-start = ((), (), s32[]{:S(2)}) async-start(), calls=%async_computation.1 | async-start | bytes 1572864 | tf_op jit(solution)/shard_map/all_gather | solution.py:152
  67.5 855.9 %reduce-scatter.2.cloned.1.call-start = ((), (), s32[]{:S(2)}) async-start(), calls=%async_computation.2 | async-start | bytes 17825792 | tf_op jit(solution)/shard_map/reduce_scatter | solution.py:153
  568.0 13.0 %copy-start.51 = (f32[2,8]{1,0:T(2,128)}, f32[2,8]{1,0:T(2,128)S(1)}, u32[]{:S(2)}) copy-start(f32[2,8]{1,0:T(2,128)S(1)} %get-tuple-element.722) | copy-start | bytes 196
  580.9 346.7 %copy-start.9 = (f32[8,2,64,64]{3,2,1,0:T(8,128)S(1)}, f32[8,2,64,64]{3,2,1,0:T(8,128)}, u32[]{:S(2)}) copy-start(f32[8,2,64,64]{3,2,1,0:T(8,128)} %copy-done.8) | copy-start | bytes 786436
  580.9 350.3 %copy-start.48 = (f32[8,2]{0,1:T(2,128)S(1)}, f32[8,2]{0,1:T(2,128)}, u32[]{:S(2)}) copy-start(f32[8,2]{0,1:T(2,128)} %slice_reduce_fusion) | copy-start | bytes 196
  580.9 356.1 %copy-start.13 = (f32[16,8,8,128]{3,2,1,0:T(8,128)S(1)}, f32[16,8,8,128]{3,2,1,0:T(8,128)}, u32[]{:S(2)}) copy-start(f32[16,8,8,128]{3,2,1,0:T(8,128)} %copy-done.12) | copy-start | bytes 1572868
  581.0 358.3 %copy-start.19 = (f32[8,2,64,64]{3,2,1,0:T(8,128)S(1)}, f32[8,2,64,64]{3,2,1,0:T(8,128)}, u32[]{:S(2)}) copy-start(f32[8,2,64,64]{3,2,1,0:T(8,128)} %copy-done.18) | copy-start | bytes 786436
  581.0 359.3 %copy-start.17 = (f32[8,2,64,64]{2,3,1,0:T(8,128)S(1)}, f32[8,2,64,64]{2,3,1,0:T(8,128)}, u32[]{:S(2)}) copy-start(f32[8,2,64,64]{2,3,1,0:T(8,128)} %copy-done.16) | copy-start | bytes 786436
  581.0 360.0 %copy-start.7 = (f32[8,2,64,64]{3,2,1,0:T(8,128)S(1)}, f32[8,2,64,64]{3,2,1,0:T(8,128)}, u32[]{:S(2)}) copy-start(f32[8,2,64,64]{3,2,1,0:T(8,128)} %copy-done.6) | copy-start | bytes 786436
  581.0 486.1 %all-gather.13.cloned.1.call-start = ((), (), s32[]{:S(2)}) async-start(), calls=%async_computation.3 | async-start | bytes 8912896 | tf_op jit(solution)/shard_map/all_gather | solution.py:159
  925.5 18.6 %copy-start.4 = (f32[8,2,64,64]{3,2,1,0:T(8,128)S(1)}, f32[8,2,64,64]{3,2,1,0:T(8,128)}, u32[]{:S(2)}) copy-start(f32[8,2,64,64]{3,2,1,0:T(8,128)} %copy-done.3) | copy-start | bytes 786436
  931.2 11.8 %copy-start.27 = (f32[8,2,64,64]{3,2,1,0:T(8,128)S(1)}, f32[8,2,64,64]{3,2,1,0:T(8,128)}, u32[]{:S(2)}) copy-start(f32[8,2,64,64]{3,2,1,0:T(8,128)} %copy-done.26) | copy-start | bytes 786436
  937.1 10.7 copy-start.25
  943.0 9.8 copy-start.11
  951.8 11.4 %copy-start.44 = (f32[8,2,64]{2,1,0:T(2,128)S(1)}, f32[8,2,64]{2,1,0:T(2,128)}, u32[]{:S(2)}) copy-start(f32[8,2,64]{2,1,0:T(2,128)} %get-tuple-element.1012) | copy-start | bytes 12292
  953.9 12.9 %copy-start.28 = (f32[2,8,128,64]{2,3,0,1:T(8,128)S(1)}, f32[2,8,128,64]{2,3,0,1:T(8,128)}, u32[]{:S(2)}) copy-start(f32[2,8,128,64]{2,3,0,1:T(8,128)} %get-tuple-element.719) | copy-start | bytes 1572868
  953.9 12.9 %copy-start.30 = (f32[2,8,64,64]{2,3,0,1:T(8,128)S(1)}, f32[2,8,64,64]{2,3,0,1:T(8,128)}, u32[]{:S(2)}) copy-start(f32[2,8,64,64]{2,3,0,1:T(8,128)} %get-tuple-element.718) | copy-start | bytes 786436
  953.9 12.9 %copy-start.35 = (f32[8,2,64,128]{3,2,1,0:T(8,128)S(1)}, f32[8,2,64,128]{3,2,1,0:T(8,128)}, u32[]{:S(2)}) copy-start(f32[8,2,64,128]{3,2,1,0:T(8,128)} %get-tuple-element.1014) | copy-start | bytes 1572868
  956.6 12.8 %copy-start.36 = (f32[2,8,64,128]{3,2,1,0:T(8,128)S(1)}, f32[2,8,64,128]{3,2,1,0:T(8,128)}, u32[]{:S(2)}) copy-start(f32[2,8,64,128]{3,2,1,0:T(8,128)} %get-tuple-element.717) | copy-start | bytes 1572868
  (27 other events, 174.4 us)
Sparse Core Ops, SparseCore 0:
  48.4 115.5 all-gather.18
  166.7 111.0 all-gather.20
  280.5 111.0 all-gather.16
  394.2 111.0 all-gather.14
  506.6 7.2 all-gather.10
  581.1 342.2 reduce-scatter.1
  926.1 140.9 all-gather.12
where the time goes:
time: 1100 us; the launch traced here: 1090 us
  waiting for transfers between devices  866 us (79%)
  matrix products  143 us (13%)
  local copies, waits for them, and re-layouts  49.4 us (4%)
  between operations  15.8 us (1%)
    all_gather x4, waiting for transfers between devices, carried_in(): gathered = jax.tree.map(lambda a: lax.all_gather(a, axis), part)  427 us
    reduce_scatter x1, waiting for transfers between devices, shards(): lax.psum_scatter(jnp.einsum('tc,th->ch', all_features, grad_value, prefer...  342 us
    dot_general x90, matrix products, product(): return jnp.matmul(left_side, right_side, precision=HIGHEST_PRECISION)  134 us
    all_gather x1, waiting for transfers between devices, shards(): grad_weight = lax.all_gather(own_rows, 'seq', axis=0, tiled=True)  95.4 us
  transfers between devices with their start and end apart: 7, of which 6 were waited for; matrix products, arithmetic and copies ran while one was open for 13% of the time, Pallas kernels for 0%

commit v1 on v0

v1 whole, which is shorter than its diff:
```python
from functools import partial

import jax
import jax.numpy as jnp
from jax import lax
from jax.experimental import pallas as pl
from jax.experimental.pallas import tpu as pltpu
from jax.sharding import PartitionSpec as P

f32 = jnp.float32
bf16 = jnp.bfloat16
PAD = 16
VMEM_LIMIT = 48 * 1024 * 1024

NN = (((1,), (0,)), ((), ()))
NT = (((1,), (1,)), ((), ()))
TN = (((0,), (0,)), ((), ()))


def dot(a, b, dims):
    return lax.dot_general(a, b, dims, preferred_element_type=f32)


def split(x):
    hi = x.astype(bf16)
    return hi, (x - hi.astype(f32)).astype(bf16)


def join(parts, axis):
    return jnp.concatenate(parts, axis=axis)


def mm(a, b, dims):
    (ca,), (cb,) = dims[0]
    if isinstance(a, tuple) and isinstance(b, tuple):
        return dot(join([a[0], a[1]], ca), join([b[0], b[0]], cb), dims) + dot(a[0], b[1], dims)
    if isinstance(a, tuple):
        return dot(join([a[0], a[1]], ca), join([b, b], cb), dims)
    if isinstance(b, tuple):
        return dot(join([a, a], ca), join([b[0], b[1]], cb), dims)
    return dot(a, b, dims)


def thirds(x):
    one = x.astype(bf16)
    rest = x - one.astype(f32)
    two = rest.astype(bf16)
    return one, two, (rest - two.astype(f32)).astype(bf16)


def pack_scalars(first, second):
    pieces = [p.astype(f32) for p in thirds(first) + thirds(second)]
    rows, width = first.shape
    out = []
    for r in range(rows):
        lines = [p[r : r + 1] for p in pieces] + [jnp.zeros((PAD - 6, width), f32)]
        out.append(jnp.concatenate(lines, axis=0).astype(bf16))
    return out


def unpack_scalars(tile):
    t = tile.astype(f32)
    return t[0:1] + t[1:2] + t[2:3], t[3:4] + t[4:5] + t[5:6]


def iotas(size):
    return (
        lax.broadcasted_iota(jnp.int32, (size, size), 0),
        lax.broadcasted_iota(jnp.int32, (size, size), 1),
    )


def turn_kernel(x_ref, out_ref):
    out_ref[...] = jnp.transpose(x_ref[...])


def pack_kernel(q_ref, k_ref, v_ref, g_ref, beta_ref, gate_ref, out_ref):
    length, heads = beta_ref.shape
    width = q_ref.shape[1] // heads
    scalars = pack_scalars(jnp.transpose(beta_ref[...]), jnp.transpose(gate_ref[...]))
    for h in range(heads):
        for place, ref in enumerate((q_ref, k_ref, v_ref, g_ref)):
            out_ref[h, pl.ds(place * length, length), :] = ref[:, pl.ds(h * width, width)]
        out_ref[h, pl.ds(4 * length, PAD), :] = scalars[h]


def scalars_of(slab_ref, count, length):
    betas, gates = [], []
    for c in range(count):
        b, g = unpack_scalars(slab_ref[c, pl.ds(4 * length, PAD), :])
        betas.append(b)
        gates.append(g)
    beta = jnp.concatenate(betas, axis=0)
    gate = jnp.concatenate(gates, axis=0)
    line, col = iotas(length)
    upper = (line <= col).astype(f32)
    running = lax.dot_general(
        gate, upper, NN, precision=lax.Precision.HIGHEST, preferred_element_type=f32
    )
    return running, jnp.transpose(running), jnp.transpose(beta)


def decay_of(run_col, run_row, causal):
    return jnp.where(causal, jnp.exp(jnp.where(causal, run_col - run_row, 0.0)), 0.0)


def first_kernel(slab_ref, maps_ref, aux_ref, ends_ref, inv_ref, low_ref):
    count = slab_ref.shape[0]
    width = slab_ref.shape[2]
    length = (slab_ref.shape[1] - PAD) // 4
    running, run_cols, beta_cols = scalars_of(slab_ref, count, length)
    line, col = iotas(length)
    causal = line >= col
    strict = line > col
    eye = (line == col).astype(f32)

    def part(c, place):
        return slab_ref[c, pl.ds(place * length, length), :]

    for c in range(count):
        decay = decay_of(run_cols[:, c : c + 1], running[c : c + 1, :], causal)
        k = part(c, 1)
        low = jnp.where(strict, beta_cols[:, c : c + 1] * decay * dot(k, k, NT), 0.0)
        low_ref[c] = low
        inv_ref[c] = eye - jnp.where((line ^ col) == 1, low, 0.0)
    size = 2
    while size < length:
        mask = ((line // size) ^ (col // size)) == 1
        for c in range(count):
            inv = split(inv_ref[c])
            side = split(jnp.where(mask, low_ref[c], 0.0))
            mid = split(mm(side, inv, NN))
            inv_ref[c] = inv_ref[c] - mm(inv, mid, NN)
        size = size * 2

    for c in range(count):
        run_col = run_cols[:, c : c + 1]
        beta = beta_cols[:, c : c + 1]
        grow = jnp.exp(run_col)
        last = running[c : c + 1, length - 1 : length]
        tail = jnp.exp(last - run_col)
        decay = decay_of(run_col, running[c : c + 1, :], causal)
        q, k, v, g = (part(c, i) for i in range(4))
        qf, kf, vf, gf = (a.astype(f32) for a in (q, k, v, g))
        inv = split(inv_ref[c])
        pairs = split(decay * dot(q, k, NT))
        both = mm(inv, split(join([(beta * grow) * kf, beta * vf], 1)), NN)
        aux_ref[c, 0] = both[:, :width]
        aux_ref[c, 1] = both[:, width:]
        moved = mm(k, split(tail * both), TN)
        eye_d = (
            lax.broadcasted_iota(jnp.int32, (width, width), 0)
            == lax.broadcasted_iota(jnp.int32, (width, width), 1)
        ).astype(f32)
        maps_ref[c, 0] = jnp.exp(last) * eye_d - moved[:, :width]
        maps_ref[c, 1] = moved[:, width:]
        back = mm(inv, split(join([mm(pairs, g, TN), tail * kf], 1)), TN)
        aux_ref[c, 2] = back[:, :width]
        aux_ref[c, 3] = back[:, width:]
        maps_ref[c, 2] = mm(g, split(grow * qf), TN) - mm(split((beta * grow) * back[:, :width]), k, TN)

    state = maps_ref[0, 1]
    adjoint = maps_ref[count - 1, 2]
    total = maps_ref[0, 0]
    for c in range(1, count):
        trans = split(maps_ref[c, 0])
        state = mm(trans, split(state), NN) + maps_ref[c, 1]
        total = mm(trans, split(total), NN)
        r = count - 1 - c
        adjoint = mm(split(adjoint), split(maps_ref[r, 0]), NN) + maps_ref[r, 2]
    ends_ref[0] = state
    ends_ref[1] = adjoint
    ends_ref[2] = total


def second_kernel(slab_ref, maps_ref, aux_ref, start_ref, finish_ref, dv_ref, out_ref, state_ref, adj_ref):
    count = slab_ref.shape[0]
    width = slab_ref.shape[2]
    length = (slab_ref.shape[1] - PAD) // 4
    running, run_cols, beta_cols = scalars_of(slab_ref, count, length)
    line, col = iotas(length)
    causal = line >= col
    strict = line > col

    state_ref[0] = start_ref[...]
    adj_ref[count - 1] = finish_ref[...]
    for c in range(1, count):
        state_ref[c] = mm(split(maps_ref[c - 1, 0]), split(state_ref[c - 1]), NN) + maps_ref[c - 1, 1]
        r = count - 1 - c
        adj_ref[r] = mm(split(adj_ref[r + 1]), split(maps_ref[r + 1, 0]), NN) + maps_ref[r + 1, 2]

    grad_beta, grad_run, consts = [], [], []
    for c in range(count):
        run_col = run_cols[:, c : c + 1]
        beta = beta_cols[:, c : c + 1]
        grow = jnp.exp(run_col)
        last = running[c : c + 1, length - 1 : length]
        tail = jnp.exp(last - run_col)
        decay = decay_of(run_col, running[c : c + 1, :], causal)
        q, k, v, g = (slab_ref[c, pl.ds(i * length, length), :] for i in range(4))
        qf, kf, vf = (a.astype(f32) for a in (q, k, v))
        state = state_ref[c]
        adj = adj_ref[c]
        state_s, adj_s = split(state), split(adj)
        update = aux_ref[c, 1] - mm(split(aux_ref[c, 0]), state_s, NN)
        update_s = split(update)
        d_rhs = aux_ref[c, 2] + mm(split(aux_ref[c, 3]), adj_s, NT)
        d_rhs_s = split(d_rhs)
        d_pair = decay * mm(g, update_s, NT)
        d_low = jnp.where(strict, -decay * mm(d_rhs_s, update_s, NT), 0.0)
        dq = grow * mm(g, state_s, NT) + mm(split(d_pair), k, NN)
        row = mm(split(d_low), k, NN) - grow * mm(d_rhs_s, state_s, NT)
        dk_row = beta * row
        wrote = tail * mm(update_s, adj_s, NN)
        dk_col = wrote + mm(split(join([d_pair, beta * d_low], 0)), join([q, k], 0), TN)
        dv_ref[c] = (beta * d_rhs).astype(bf16)
        out_ref[c, pl.ds(0, length), :] = dq.astype(bf16)
        out_ref[c, pl.ds(length, length), :] = (dk_row + dk_col).astype(bf16)
        grad_beta.append(jnp.sum(d_rhs * vf + kf * row, axis=1, keepdims=True))
        grad_run.append(jnp.sum(qf * dq + kf * (dk_row - dk_col), axis=1, keepdims=True))
        carry = jnp.exp(last) * jnp.sum(state * jnp.transpose(adj)) + jnp.sum(kf * wrote)
        consts.append(carry)
    db = jnp.concatenate(grad_beta, axis=1)
    dr = jnp.concatenate(grad_run, axis=1)
    upper = (line <= col).astype(f32)
    dg = lax.dot_general(
        upper, dr, NN, precision=lax.Precision.HIGHEST, preferred_element_type=f32
    ) + jnp.concatenate(consts, axis=1)
    packed = pack_scalars(jnp.transpose(db), jnp.transpose(dg))
    for c in range(count):
        out_ref[c, pl.ds(2 * length, PAD), :] = packed[c]


def swap(x, mask):
    return lax.ppermute(x, "seq", [(i, i ^ mask) for i in range(lax.axis_size("seq"))])


def gather_parts(x):
    half = x.shape[0] // 2
    out = []
    far = [(m, swap(x, m) if m else x) for m in range(0, lax.axis_size("seq"), 4)]
    for m, own in far:
        side, down = swap(own, 1), swap(own, 2)
        out += [(m, 0, own), (m | 1, 0, side), (m | 2, 0, down)]
        out += [(m | 3, 0, swap(down[:half], 1)), (m | 3, half, swap(side[half:], 2))]
    return out


def place_kernel(where, place_ref, *refs):
    parts, (all_ref, rows_ref) = refs[: len(where)], refs[len(where) :]
    shards, count, length, width = all_ref.shape
    heads = rows_ref.shape[1] // width
    me = place_ref[0]
    for (mask, first), part in zip(where, parts):
        all_ref[me ^ mask, pl.ds(first, part.shape[0])] = part[...]
    group = me // heads * heads
    for h in range(heads):
        rows_ref[:, pl.ds(h * width, width)] = all_ref[group + h, me - group]


def unpack_kernel(back_ref, dq_ref, dk_ref, dbeta_ref, dgate_ref):
    heads = back_ref.shape[0]
    length, width = dq_ref.shape[0], dq_ref.shape[1] // heads
    betas, gates = [], []
    for h in range(heads):
        lanes = pl.ds(h * width, width)
        dq_ref[:, lanes] = back_ref[h, pl.ds(0, length), :]
        dk_ref[:, lanes] = back_ref[h, pl.ds(length, length), :]
        b, g = unpack_scalars(back_ref[h, pl.ds(2 * length, PAD), :])
        betas.append(b)
        gates.append(g)
    dbeta_ref[...] = jnp.transpose(jnp.concatenate(betas, axis=0))
    dgate_ref[...] = jnp.transpose(jnp.concatenate(gates, axis=0))


def weight_kernel(x_ref, dv_ref, out_ref):
    shards = x_ref.shape[0]
    groups, heads, count = dv_ref.shape[:3]
    total = None
    step = 2 if count % 2 == 0 else 1
    for s in range(0, shards, step):
        left = join([x_ref[s + i, 0] for i in range(step)], 1)
        right = join(
            [join([dv_ref[(s + i) // count, h, (s + i) % count] for h in range(heads)], 1) for i in range(step)], 0
        )
        term = dot(left, right, NN)
        total = term if total is None else total + term
    out_ref[...] = total.astype(out_ref.dtype)


def weight_grad(x_all, dv_all, block):
    shards, halves, feats, length = x_all.shape
    groups, heads, count, _, width = dv_all.shape
    per = feats // block
    return pl.pallas_call(
        weight_kernel,
        grid=(halves * per,),
        in_specs=[
            pl.BlockSpec((shards, 1, block, length), lambda i: (0, i // per, i % per, 0)),
            pl.BlockSpec(dv_all.shape, lambda i: (0, 0, 0, 0, 0)),
        ],
        out_specs=pl.BlockSpec((block, heads * width), lambda i: (i, 0)),
        out_shape=jax.ShapeDtypeStruct((halves * feats, heads * width), bf16),
        compiler_params=pltpu.CompilerParams(vmem_limit_bytes=VMEM_LIMIT),
    )(x_all, dv_all)


def whole_call(kernel, outs, scratch=(), flops=0):
    return pl.pallas_call(
        kernel,
        out_shape=[jax.ShapeDtypeStruct(s, d) for s, d in outs],
        scratch_shapes=[pltpu.VMEM(s, d) for s, d in scratch],
        compiler_params=pltpu.CompilerParams(vmem_limit_bytes=VMEM_LIMIT),
    )


def shards(layer_input, query_rows, key_matrix_rows, value_rows, beta_rows, log_gate, grad_out):
    length, heads = beta_rows.shape
    width = query_rows.shape[1] // heads
    seq = lax.axis_size("seq")
    halves = lax.axis_size("head")
    groups = seq // heads
    count = heads
    members = [[g * heads + i for i in range(heads)] for g in range(groups)]

    slabs = whole_call(pack_kernel, [((heads, 4 * length + PAD, width), bf16)])(
        query_rows, key_matrix_rows, value_rows, grad_out, beta_rows, log_gate
    )[0]
    slabs = lax.all_to_all(slabs, "seq", 0, 0, axis_index_groups=members, tiled=True)
    turned = whole_call(turn_kernel, [(layer_input.shape[::-1], bf16)])(layer_input)[0]
    x_all = lax.all_gather(turned, ("seq", "head"), axis=0).reshape(
        (seq, halves) + turned.shape
    )

    square = (width, width)
    maps, aux, ends = whole_call(
        first_kernel,
        [((count, 3) + square, f32), ((count, 4, length, width), f32), ((3,) + square, f32)],
        [((count, length, length), f32), ((count, length, length), f32)],
    )(slabs)
    up = [(s, s + heads) for s in range(seq - heads)]
    down = [(s + heads, s) for s in range(seq - heads)]
    start = lax.ppermute(ends[0], "seq", up)
    finish = lax.ppermute(ends[1], "seq", down)
    for _ in range(groups - 2):
        start = lax.ppermute(
            jnp.matmul(ends[2], start, precision=lax.Precision.HIGHEST) + ends[0], "seq", up
        )
        finish = lax.ppermute(
            jnp.matmul(finish, ends[2], precision=lax.Precision.HIGHEST) + ends[1], "seq", down
        )

    dv, grads = whole_call(
        second_kernel,
        [((count, length, width), bf16), ((count, 2 * length + PAD, width), bf16)],
        [((count,) + square, f32), ((count,) + square, f32)],
    )(slabs, maps, aux, start, finish)
    back = lax.all_to_all(grads, "seq", 0, 0, axis_index_groups=members, tiled=True)

    rows = (length, heads * width)
    parts = gather_parts(dv)
    me = lax.axis_index("seq").astype(jnp.int32).reshape(1)
    vmem = pl.BlockSpec(memory_space=pltpu.VMEM)
    dv_all, dvo = pl.pallas_call(
        partial(place_kernel, [p[:2] for p in parts]),
        in_specs=[pl.BlockSpec(memory_space=pltpu.SMEM)] + [vmem] * len(parts),
        out_specs=[vmem, vmem],
        out_shape=[
            jax.ShapeDtypeStruct((seq, count, length, width), bf16),
            jax.ShapeDtypeStruct(rows, bf16),
        ],
        compiler_params=pltpu.CompilerParams(vmem_limit_bytes=VMEM_LIMIT),
    )(me, *[p[2] for p in parts])
    dv_all = dv_all.reshape(groups, heads, count, length, width)
    dq, dk, dbeta, dgate = whole_call(
        unpack_kernel, [(rows, bf16), (rows, bf16), ((length, heads), f32), ((length, heads), f32)]
    )(back)
    weight = weight_grad(x_all, dv_all, min(512, layer_input.shape[1]))
    return dq, dk, dvo, dbeta, dgate, weight


def solution(mesh):
    row = P("seq", "head")
    return jax.shard_map(
        shards, mesh=mesh, in_specs=(row,) * 7, out_specs=(row,) * 5 + (P(None, "head"),), check_vma=False
    )
```

time: 1100 us -> 196 us (0.18); the launches traced: 1090 us -> 196 us
  waiting for transfers between devices: 866 us -> 53.7 us
  matrix products: 143 us -> 0 us
  Pallas kernels: 0 us -> 43 us
  blocking collectives: 0 us -> 32.9 us
  starting transfers between devices: 0.45 us -> 33.1 us
  local copies, waits for them, and re-layouts: 49.4 us -> 19 us
    all_gather x6 -> x1, waiting for transfers between devices: 523 us -> 0.01 us  [shards(): lax.all_gather(turned, ('seq', 'head'), axis=0)]
    reduce_scatter x1 -> x0, waiting for transfers between devices: 342 us -> none  [shards(): lax.psum_scatter(jnp.einsum('tc,th->ch', all_features, grad_value, prefer...]
    dot_general x91 -> x0, matrix products: 143 us -> none  [the longest x90 134 us: product(): return jnp.matmul(left_side, right_side, precision=HIGHEST_PRECISION)]
    ppermute x0 -> x21, waiting for transfers between devices: none -> 53.7 us  [the longest x19 49.4 us: swap(): lax.ppermute(x, 'seq', [(i, i ^ mask) for i in range(lax.axis_size('seq'))])]
    pallas_call x0 -> x7, Pallas kernels: none -> 43 us  [the longest x1 21.4 us: weight_grad(): pl.pallas_call(weight_kernel, grid=(halves * per,), in_specs=[pl.BlockSpe...]
    all_to_all x0 -> x1, blocking collectives: none -> 32.9 us  [shards(): lax.all_to_all(slabs, 'seq', 0, 0, axis_index_groups=members, tiled=True)]
    ppermute x0 -> x21, starting transfers between devices: none -> 29.5 us  [the longest x19 22.6 us: swap(): lax.ppermute(x, 'seq', [(i, i ^ mask) for i in range(lax.axis_size('seq'))])]
  transfers between devices with their start and end apart: 7 -> 23, of which waited for: 6 -> 10; matrix products, arithmetic and copies ran while one was open for 13% -> 3% of each run, Pallas kernels for 0% -> 11%
where the time goes in v1:
time: 196 us
  waiting for transfers between devices  53.7 us (27%)
  Pallas kernels  43 us (22%)
  starting transfers between devices  33.1 us (17%)
  blocking collectives  32.9 us (17%)
  local copies, waits for them, and re-layouts  19 us (10%)
  between operations  14.1 us (7%)
    ppermute x19, waiting for transfers between devices, swap(): lax.ppermute(x, 'seq', [(i, i ^ mask) for i in range(lax.axis_size('seq'))])  49.4 us
    all_to_all x1, blocking collectives, shards(): lax.all_to_all(slabs, 'seq', 0, 0, axis_index_groups=members, tiled=True)  32.9 us
    ppermute x19, starting transfers between devices, swap(): lax.ppermute(x, 'seq', [(i, i ^ mask) for i in range(lax.axis_size('seq'))])  22.6 us
    pallas_call x1, Pallas kernels, weight_grad(): pl.pallas_call(weight_kernel, grid=(halves * per,), in_specs=[pl.BlockSpe...  21.4 us
    unnamed x32, local copies, waits for them, and re-layouts  15.6 us
    pallas_call x1, Pallas kernels, shards(): whole_call(first_kernel, [((count, 3) + square, f32), ((count, 4, length,...  9.08 us
    pallas_call x1, Pallas kernels, shards(): whole_call(second_kernel, [((count, length, width), bf16), ((count, 2 * l...  6.84 us
    ppermute x1, starting transfers between devices, shards(): start = lax.ppermute(ends[0], 'seq', up)  5.63 us
  transfers between devices with their start and end apart: 23, of which 10 were waited for; matrix products, arithmetic and copies ran while one was open for 3% of the time, Pallas kernels for 11%

profile of v1, /device:TPU:0, one launch (start us, length us, event | category | flops | bytes accessed | tf_op | source)
XLA Modules:
  0.0 195.7 jit_solution(5559598811355315186)
XLA Ops:
  7.2 1.0 copy-done.1
  8.3 1.0 shard_map.123
  14.9 32.9 %all_to_all.10.slab_ref = bf16[8,528,128]{2,1,0:T(8,128)(2,1)S(1)} all-to-all(bf16[8,528,128]{2,1,0:T(8,128)(2,1)S(1)} %shard_map.118), channel_id=1, replica_groups={{0,2,4,6,8,10,12,14},{16,18,20,22,24,26,28,30},{1,3,5,7,9,11,13,15},{17..., dimensions={0} | all-to-all | bytes 2162688 | tf_op jit(solution)/shard_map/all_to_all | solution.py:329
  47.8 9.1 %shard_map.119 = (f32[8,3,128,128]{3,2,1,0:T(8,128)S(1)}, f32[8,4,128,128]{3,2,1,0:T(8,128)S(1)}, f32[3,128,128]{2,1,0:T(8,128)S(1)}) custom-call(bf16[8,528,128]{2,1,0:T(8,128)(2,1)S(1)} %all_to_all.10.slab_ref), custom_call_target="tpu_custom_call" | custom-call | tf_op jit(solution)/shard_map/pallas_call | solution.py:336
  56.9 1.3 collective-permute-start.1
  58.2 5.6 %collective-permute-start = (f32[128,128]{1,0:T(8,128)S(1)}, f32[128,128]{1,0:T(8,128)S(1)}, u32[]{:S(2)}, u32[]{:S(2)}) collective-permute-start(f32[128,128]{1,0:T(8,128)S(1)} %get-tuple-element.35), channel_id=1, source_target_pairs={{0,16},{2,18},{4,20},{6,22},{8,24},{10,26},{12,28},{14,30},{1,17},... | collective-permute-start | bytes 196616 | tf_op jit(solution)/shard_map/ppermute | solution.py:343
  63.8 4.3 %collective-permute-done.1.finish_ref = f32[128,128]{1,0:T(8,128)S(1)} collective-permute-done((f32[128,128]{1,0:T(8,128)S(1)}, f32[128,128]{1,0:T(8,128)S(1)}, u32[]{:S(2)}, u32[]{:S(2)}) %collective-permute-start.1) | collective-permute-done | bytes 65568 | tf_op jit(solution)/shard_map/ppermute | solution.py:344
  68.1 6.8 %shard_map.120 = (bf16[8,128,128]{2,1,0:T(8,128)(2,1)S(1)}, bf16[8,272,128]{2,1,0:T(8,128)(2,1)}) custom-call(bf16[8,528,128]{2,1,0:T(8,128)(2,1)S(1)} %all_to_all.10.slab_ref, f32[8,3,128,128]{3,2,1,0:T(8,128)S(1)} %get-tuple-element.17.maps_ref, f32[8,4,128,128]{3,2,1,0:T(8,128)S(1)} %get-tuple-element.18.aux_ref, ...), custom_call_target="tpu_custom_call" | custom-call | tf_op jit(solution)/shard_map/pallas_call | solution.py:353
  74.9 3.5 %all-to-all-start.1 = ((bf16[8,272,128]{2,1,0:T(8,128)(2,1)}), bf16[8,272,128]{2,1,0:T(8,128)(2,1)S(1)}, u32[]{:S(2)}, u32[]{:S(2)}) async-start(bf16[8,272,128]{2,1,0:T(8,128)(2,1)} %get-tuple-element.20), calls=%async_computation.1 | async-start | bytes 1114112 | tf_op jit(solution)/shard_map/all_to_all | solution.py:358
  78.5 4.7 %collective-permute-start.16 = (bf16[8,128,128]{2,1,0:T(8,128)(2,1)S(1)}, bf16[8,128,128]{2,1,0:T(8,128)(2,1)S(1)}, u32[]{:S(2)}, u32[]{:S(2)}) collective-permute-start(bf16[8,128,128]{2,1,0:T(8,128)(2,1)S(1)} %get-tuple-element.23.refs_0_), channel_id=1, source_target_pairs={{0,24},{2,26},{4,28},{6,30},{8,16},{10,18},{12,20},{14,22},{16,8},... | collective-permute-start | bytes 786440 | tf_op jit(solution)/shard_map/ppermute | solution.py:235
  83.8 1.5 collective-permute-start.3
  85.2 1.5 collective-permute-start.2
  86.7 17.1 %collective-permute-done.16.refs_15_ = bf16[8,128,128]{2,1,0:T(8,128)(2,1)S(1)} collective-permute-done((bf16[8,128,128]{2,1,0:T(8,128)(2,1)S(1)}, bf16[8,128,128]{2,1,0:T(8,128)(2,1)S(1)}, u32[]{:S(2)}, u32[]{:S(2)}) %collective-permute-start.16) | collective-permute-done | bytes 262176 | tf_op jit(solution)/shard_map/ppermute | solution.py:235
  103.8 1.5 collective-permute-start.18
  105.3 15.8 %collective-permute-done.11.refs_10_ = bf16[8,128,128]{2,1,0:T(8,128)(2,1)S(1)} collective-permute-done((bf16[8,128,128]{2,1,0:T(8,128)(2,1)S(1)}, bf16[8,128,128]{2,1,0:T(8,128)(2,1)S(1)}, u32[]{:S(2)}, u32[]{:S(2)}) %collective-permute-start.11) | collective-permute-done | bytes 262176 | tf_op jit(solution)/shard_map/ppermute | solution.py:235
  121.1 2.0 %collective-permute-start.17 = (bf16[8,128,128]{2,1,0:T(8,128)(2,1)S(1)}, bf16[8,128,128]{2,1,0:T(8,128)(2,1)S(1)}, u32[]{:S(2)}, u32[]{:S(2)}) collective-permute-start(bf16[8,128,128]{2,1,0:T(8,128)(2,1)S(1)} %collective-permute-done.16.refs_15_), channel_id=1, source_target_pairs={{0,2},{2,0},{4,6},{6,4},{8,10},{10,8},{12,14},{14,12},{16,18},{18,... | collective-permute-start | bytes 786440 | tf_op jit(solution)/shard_map/ppermute | solution.py:235
  123.1 1.5 collective-permute-start.13
  125.2 1.9 collective-permute-start.7
  127.2 5.6 %collective-permute-done.17.refs_16_ = bf16[8,128,128]{2,1,0:T(8,128)(2,1)S(1)} collective-permute-done((bf16[8,128,128]{2,1,0:T(8,128)(2,1)S(1)}, bf16[8,128,128]{2,1,0:T(8,128)(2,1)S(1)}, u32[]{:S(2)}, u32[]{:S(2)}) %collective-permute-start.17) | collective-permute-done | bytes 262176 | tf_op jit(solution)/shard_map/ppermute | solution.py:235
  132.8 1.0 collective-permute-start.4
  133.8 3.7 %collective-permute-done.13.refs_12_ = bf16[8,128,128]{2,1,0:T(8,128)(2,1)S(1)} collective-permute-done((bf16[8,128,128]{2,1,0:T(8,128)(2,1)S(1)}, bf16[8,128,128]{2,1,0:T(8,128)(2,1)S(1)}, u32[]{:S(2)}, u32[]{:S(2)}) %collective-permute-start.13) | collective-permute-done | bytes 262176 | tf_op jit(solution)/shard_map/ppermute | solution.py:235
  138.5 1.0 collective-permute-start.19
  141.4 1.7 collective-permute-done.8.refs_7_
  146.4 1.0 collective-permute-start.15
  148.1 1.7 collective-permute-start.9
  151.7 1.7 collective-permute-done.9.refs_8_
  153.3 2.4 %collective-permute-done.10.refs_9_ = bf16[4,128,128]{2,1,0:T(8,128)(2,1)} collective-permute-done((bf16[4,128,128]{2,1,0:T(8,128)(2,1)}, bf16[4,128,128]{2,1,0:T(8,128)(2,1)}, u32[]{:S(2)}, u32[]{:S(2)}) %collective-permute-start.10) | collective-permute-done | bytes 131104 | tf_op jit(solution)/shard_map/ppermute | solution.py:235
  155.8 0.9 copy-done.7
  156.7 1.0 copy-done.9
  159.5 3.5 %shard_map.122 = (bf16[16,8,128,128]{3,2,1,0:T(8,128)(2,1)}, bf16[128,1024]{1,0:T(8,128)(2,1)}) custom-call(s32[1]{0:T(128)} %bitcast.2.place_ref, bf16[8,128,128]{2,1,0:T(8,128)(2,1)S(1)} %get-tuple-element.23.refs_0_, bf16[8,128,128]{2,1,0:T(8,128)(2,1)S(1)} %collective-permute-done.2.refs_1_, bf16[8,128,128]{2,1,0:T(8,128)(2,1)S(1)} %collective-permute-done.3.refs_2_, ...), custom_call_target="tpu_custom_call" | custom-call | tf_op jit(solution)/shard_map/pallas_call | solution.py:364
  165.2 2.2 %copy-done = bf16[16,8,128,128]{3,2,1,0:T(8,128)(2,1)S(1)} copy-done((bf16[16,8,128,128]{3,2,1,0:T(8,128)(2,1)S(1)}, bf16[16,8,128,128]{3,2,1,0:T(8,128)(2,1)}, u32[]{:S(2)}) %copy-start) | copy-done | bytes 4194328
  167.4 21.4 %shard_map.124 = bf16[4096,1024]{1,0:T(8,128)(2,1)} custom-call(bf16[16,2,2048,128]{3,2,1,0:T(8,128)(2,1)} %bitcast.8, bf16[2,8,8,128,128]{4,3,2,1,0:T(8,128)(2,1)S(1)} %bitcast.7), custom_call_target="tpu_custom_call" | custom-call | tf_op jit(solution)/shard_map/pallas_call | solution.py:295
  (64 shorter events, 19.6 us)
Async XLA Ops:
  7.2 158.1 %all-gather.3.cloned.1.call-start = ((), (), s32[]{:S(2)}) async-start(), calls=%async_computation.2 | async-start | bytes 17301504 | tf_op jit(solution)/shard_map/all_gather | solution.py:331
  7.2 1.0 copy-start.1
  10.9 0.9 copy-start.2
  11.8 0.9 copy-start.3
  12.8 0.9 copy-start.4
  13.7 0.9 copy-start.5
  56.9 11.2 %collective-permute-start.1 = (f32[128,128]{1,0:T(8,128)S(1)}, f32[128,128]{1,0:T(8,128)S(1)}, u32[]{:S(2)}, u32[]{:S(2)}) collective-permute-start(f32[128,128]{1,0:T(8,128)S(1)} %get-tuple-element.34), channel_id=1, source_target_pairs={{16,0},{18,2},{20,4},{22,6},{24,8},{26,10},{28,12},{30,14},{17,1},... | collective-permute-start | bytes 196616 | tf_op jit(solution)/shard_map/ppermute | solution.py:344
  58.2 9.9 %collective-permute-start = (f32[128,128]{1,0:T(8,128)S(1)}, f32[128,128]{1,0:T(8,128)S(1)}, u32[]{:S(2)}, u32[]{:S(2)}) collective-permute-start(f32[128,128]{1,0:T(8,128)S(1)} %get-tuple-element.35), channel_id=1, source_target_pairs={{0,16},{2,18},{4,20},{6,22},{8,24},{10,26},{12,28},{14,30},{1,17},... | collective-permute-start | bytes 196616 | tf_op jit(solution)/shard_map/ppermute | solution.py:343
  74.9 88.1 %all-to-all-start.1 = ((bf16[8,272,128]{2,1,0:T(8,128)(2,1)}), bf16[8,272,128]{2,1,0:T(8,128)(2,1)S(1)}, u32[]{:S(2)}, u32[]{:S(2)}) async-start(bf16[8,272,128]{2,1,0:T(8,128)(2,1)} %get-tuple-element.20), calls=%async_computation.1 | async-start | bytes 1114112 | tf_op jit(solution)/shard_map/all_to_all | solution.py:358
  78.5 25.3 %collective-permute-start.16 = (bf16[8,128,128]{2,1,0:T(8,128)(2,1)S(1)}, bf16[8,128,128]{2,1,0:T(8,128)(2,1)S(1)}, u32[]{:S(2)}, u32[]{:S(2)}) collective-permute-start(bf16[8,128,128]{2,1,0:T(8,128)(2,1)S(1)} %get-tuple-element.23.refs_0_), channel_id=1, source_target_pairs={{0,24},{2,26},{4,28},{6,30},{8,16},{10,18},{12,20},{14,22},{16,8},... | collective-permute-start | bytes 786440 | tf_op jit(solution)/shard_map/ppermute | solution.py:235
  83.2 37.9 %collective-permute-start.11 = (bf16[8,128,128]{2,1,0:T(8,128)(2,1)S(1)}, bf16[8,128,128]{2,1,0:T(8,128)(2,1)S(1)}, u32[]{:S(2)}, u32[]{:S(2)}) collective-permute-start(bf16[8,128,128]{2,1,0:T(8,128)(2,1)S(1)} %get-tuple-element.23.refs_0_), channel_id=1, source_target_pairs={{0,16},{2,18},{4,20},{6,22},{8,24},{10,26},{12,28},{14,30},{16,0},... | collective-permute-start | bytes 786440 | tf_op jit(solution)/shard_map/ppermute | solution.py:235
  83.2 39.9 %collective-permute-start.6 = (bf16[8,128,128]{2,1,0:T(8,128)(2,1)S(1)}, bf16[8,128,128]{2,1,0:T(8,128)(2,1)S(1)}, u32[]{:S(2)}, u32[]{:S(2)}) collective-permute-start(bf16[8,128,128]{2,1,0:T(8,128)(2,1)S(1)} %get-tuple-element.23.refs_0_), channel_id=1, source_target_pairs={{0,8},{2,10},{4,12},{6,14},{8,0},{10,2},{12,4},{14,6},{16,24},{18,... | collective-permute-start | bytes 786440 | tf_op jit(solution)/shard_map/ppermute | solution.py:235
  83.8 40.8 %collective-permute-start.3 = (bf16[8,128,128]{2,1,0:T(8,128)(2,1)S(1)}, bf16[8,128,128]{2,1,0:T(8,128)(2,1)S(1)}, u32[]{:S(2)}, u32[]{:S(2)}) collective-permute-start(bf16[8,128,128]{2,1,0:T(8,128)(2,1)S(1)} %get-tuple-element.23.refs_0_), channel_id=1, source_target_pairs={{0,4},{2,6},{4,0},{6,2},{8,12},{10,14},{12,8},{14,10},{16,20},{18,... | collective-permute-start | bytes 786440 | tf_op jit(solution)/shard_map/ppermute | solution.py:235
  85.2 39.9 %collective-permute-start.2 = (bf16[8,128,128]{2,1,0:T(8,128)(2,1)S(1)}, bf16[8,128,128]{2,1,0:T(8,128)(2,1)S(1)}, u32[]{:S(2)}, u32[]{:S(2)}) collective-permute-start(bf16[8,128,128]{2,1,0:T(8,128)(2,1)S(1)} %get-tuple-element.23.refs_0_), channel_id=1, source_target_pairs={{0,2},{2,0},{4,6},{6,4},{8,10},{10,8},{12,14},{14,12},{16,18},{18,... | collective-permute-start | bytes 786440 | tf_op jit(solution)/shard_map/ppermute | solution.py:235
  103.8 21.4 %collective-permute-start.18 = (bf16[8,128,128]{2,1,0:T(8,128)(2,1)S(1)}, bf16[8,128,128]{2,1,0:T(8,128)(2,1)S(1)}, u32[]{:S(2)}, u32[]{:S(2)}) collective-permute-start(bf16[8,128,128]{2,1,0:T(8,128)(2,1)S(1)} %collective-permute-done.16.refs_15_), channel_id=1, source_target_pairs={{0,4},{2,6},{4,0},{6,2},{8,12},{10,14},{12,8},{14,10},{16,20},{18,... | collective-permute-start | bytes 786440 | tf_op jit(solution)/shard_map/ppermute | solution.py:235
  121.1 11.8 %collective-permute-start.17 = (bf16[8,128,128]{2,1,0:T(8,128)(2,1)S(1)}, bf16[8,128,128]{2,1,0:T(8,128)(2,1)S(1)}, u32[]{:S(2)}, u32[]{:S(2)}) collective-permute-start(bf16[8,128,128]{2,1,0:T(8,128)(2,1)S(1)} %collective-permute-done.16.refs_15_), channel_id=1, source_target_pairs={{0,2},{2,0},{4,6},{6,4},{8,10},{10,8},{12,14},{14,12},{16,18},{18,... | collective-permute-start | bytes 786440 | tf_op jit(solution)/shard_map/ppermute | solution.py:235
  123.1 21.1 %copy-start.6 = (bf16[8,128,128]{2,1,0:T(8,128)(2,1)}, bf16[8,128,128]{2,1,0:T(8,128)(2,1)S(1)}, u32[]{:S(2)}) copy-start(bf16[8,128,128]{2,1,0:T(8,128)(2,1)S(1)} %collective-permute-done.6.refs_5_) | copy-start | bytes 786436
  123.1 14.4 %collective-permute-start.13 = (bf16[8,128,128]{2,1,0:T(8,128)(2,1)S(1)}, bf16[8,128,128]{2,1,0:T(8,128)(2,1)S(1)}, u32[]{:S(2)}, u32[]{:S(2)}) collective-permute-start(bf16[8,128,128]{2,1,0:T(8,128)(2,1)S(1)} %collective-permute-done.11.refs_10_), channel_id=1, source_target_pairs={{0,4},{2,6},{4,0},{6,2},{8,12},{10,14},{12,8},{14,10},{16,20},{18,... | collective-permute-start | bytes 786440 | tf_op jit(solution)/shard_map/ppermute | solution.py:235
  124.5 13.9 %collective-permute-start.12 = (bf16[8,128,128]{2,1,0:T(8,128)(2,1)S(1)}, bf16[8,128,128]{2,1,0:T(8,128)(2,1)S(1)}, u32[]{:S(2)}, u32[]{:S(2)}) collective-permute-start(bf16[8,128,128]{2,1,0:T(8,128)(2,1)S(1)} %collective-permute-done.11.refs_10_), channel_id=1, source_target_pairs={{0,2},{2,0},{4,6},{6,4},{8,10},{10,8},{12,14},{14,12},{16,18},{18,... | collective-permute-start | bytes 786440 | tf_op jit(solution)/shard_map/ppermute | solution.py:235
  125.1 18.0 %collective-permute-start.8 = (bf16[8,128,128]{2,1,0:T(8,128)(2,1)S(1)}, bf16[8,128,128]{2,1,0:T(8,128)(2,1)S(1)}, u32[]{:S(2)}, u32[]{:S(2)}) collective-permute-start(bf16[8,128,128]{2,1,0:T(8,128)(2,1)S(1)} %collective-permute-done.6.refs_5_), channel_id=1, source_target_pairs={{0,4},{2,6},{4,0},{6,2},{8,12},{10,14},{12,8},{14,10},{16,20},{18,... | collective-permute-start | bytes 786440 | tf_op jit(solution)/shard_map/ppermute | solution.py:235
  125.2 19.0 %collective-permute-start.7 = (bf16[8,128,128]{2,1,0:T(8,128)(2,1)S(1)}, bf16[8,128,128]{2,1,0:T(8,128)(2,1)S(1)}, u32[]{:S(2)}, u32[]{:S(2)}) collective-permute-start(bf16[8,128,128]{2,1,0:T(8,128)(2,1)S(1)} %collective-permute-done.6.refs_5_), channel_id=1, source_target_pairs={{0,2},{2,0},{4,6},{6,4},{8,10},{10,8},{12,14},{14,12},{16,18},{18,... | collective-permute-start | bytes 786440 | tf_op jit(solution)/shard_map/ppermute | solution.py:235
  132.8 12.9 %collective-permute-start.4 = (bf16[4,128,128]{2,1,0:T(8,128)(2,1)S(1)}, bf16[4,128,128]{2,1,0:T(8,128)(2,1)S(1)}, u32[]{:S(2)}, u32[]{:S(2)}) collective-permute-start(bf16[4,128,128]{2,1,0:T(8,128)(2,1)S(1)} %slice.40), channel_id=1, source_target_pairs={{0,2},{2,0},{4,6},{6,4},{8,10},{10,8},{12,14},{14,12},{16,18},{18,... | collective-permute-start | bytes 393224 | tf_op jit(solution)/shard_map/ppermute | solution.py:235
  137.5 9.9 %collective-permute-start.5 = (bf16[4,128,128]{2,1,0:T(8,128)(2,1)S(1)}, bf16[4,128,128]{2,1,0:T(8,128)(2,1)S(1)}, u32[]{:S(2)}, u32[]{:S(2)}) collective-permute-start(bf16[4,128,128]{2,1,0:T(8,128)(2,1)S(1)} %slice.41), channel_id=1, source_target_pairs={{0,4},{2,6},{4,0},{6,2},{8,12},{10,14},{12,8},{14,10},{16,20},{18,... | collective-permute-start | bytes 393224 | tf_op jit(solution)/shard_map/ppermute | solution.py:235
  138.5 11.4 %collective-permute-start.19 = (bf16[4,128,128]{2,1,0:T(8,128)(2,1)S(1)}, bf16[4,128,128]{2,1,0:T(8,128)(2,1)S(1)}, u32[]{:S(2)}, u32[]{:S(2)}) collective-permute-start(bf16[4,128,128]{2,1,0:T(8,128)(2,1)S(1)} %slice.46), channel_id=1, source_target_pairs={{0,2},{2,0},{4,6},{6,4},{8,10},{10,8},{12,14},{14,12},{16,18},{18,... | collective-permute-start | bytes 393224 | tf_op jit(solution)/shard_map/ppermute | solution.py:235
  143.1 7.8 %collective-permute-start.20 = (bf16[4,128,128]{2,1,0:T(8,128)(2,1)}, bf16[4,128,128]{2,1,0:T(8,128)(2,1)}, u32[]{:S(2)}, u32[]{:S(2)}) collective-permute-start(bf16[4,128,128]{2,1,0:T(8,128)(2,1)} %slice.47), channel_id=1, source_target_pairs={{0,4},{2,6},{4,0},{6,2},{8,12},{10,14},{12,8},{14,10},{16,20},{18,... | collective-permute-start | bytes 393224 | tf_op jit(solution)/shard_map/ppermute | solution.py:235
  144.2 6.7 %collective-permute-start.14 = (bf16[4,128,128]{2,1,0:T(8,128)(2,1)}, bf16[4,128,128]{2,1,0:T(8,128)(2,1)}, u32[]{:S(2)}, u32[]{:S(2)}) collective-permute-start(bf16[4,128,128]{2,1,0:T(8,128)(2,1)} %slice.44), channel_id=1, source_target_pairs={{0,2},{2,0},{4,6},{6,4},{8,10},{10,8},{12,14},{14,12},{16,18},{18,... | collective-permute-start | bytes 393224 | tf_op jit(solution)/shard_map/ppermute | solution.py:235
  146.4 5.3 %collective-permute-start.15 = (bf16[4,128,128]{2,1,0:T(8,128)(2,1)}, bf16[4,128,128]{2,1,0:T(8,128)(2,1)}, u32[]{:S(2)}, u32[]{:S(2)}) collective-permute-start(bf16[4,128,128]{2,1,0:T(8,128)(2,1)} %slice.45), channel_id=1, source_target_pairs={{0,4},{2,6},{4,0},{6,2},{8,12},{10,14},{12,8},{14,10},{16,20},{18,... | collective-permute-start | bytes 393224 | tf_op jit(solution)/shard_map/ppermute | solution.py:235
  148.1 5.3 %collective-permute-start.9 = (bf16[4,128,128]{2,1,0:T(8,128)(2,1)}, bf16[4,128,128]{2,1,0:T(8,128)(2,1)}, u32[]{:S(2)}, u32[]{:S(2)}) collective-permute-start(bf16[4,128,128]{2,1,0:T(8,128)(2,1)} %slice.42), channel_id=1, source_target_pairs={{0,2},{2,0},{4,6},{6,4},{8,10},{10,8},{12,14},{14,12},{16,18},{18,... | collective-permute-start | bytes 393224 | tf_op jit(solution)/shard_map/ppermute | solution.py:235
  150.5 5.3 %collective-permute-start.10 = (bf16[4,128,128]{2,1,0:T(8,128)(2,1)}, bf16[4,128,128]{2,1,0:T(8,128)(2,1)}, u32[]{:S(2)}, u32[]{:S(2)}) collective-permute-start(bf16[4,128,128]{2,1,0:T(8,128)(2,1)} %slice.43), channel_id=1, source_target_pairs={{0,4},{2,6},{4,0},{6,2},{8,12},{10,14},{12,8},{14,10},{16,20},{18,... | collective-permute-start | bytes 393224 | tf_op jit(solution)/shard_map/ppermute | solution.py:235
  155.8 1.0 copy-start.7
  156.7 1.0 copy-start.9
  165.2 2.2 %copy-start = (bf16[16,8,128,128]{3,2,1,0:T(8,128)(2,1)S(1)}, bf16[16,8,128,128]{3,2,1,0:T(8,128)(2,1)}, u32[]{:S(2)}) copy-start(bf16[16,8,128,128]{3,2,1,0:T(8,128)(2,1)} %get-tuple-element.27) | copy-start | bytes 12582916
  (5 other events, 3.8 us)
Sparse Core Ops, SparseCore 0:
  10.9 147.7 all-gather.2

commit v2 on v1

--- a/solution.py
+++ b/solution.py
@@ -10,6 +10,8 @@
 f32 = jnp.float32
 bf16 = jnp.bfloat16
 PAD = 16
+PLAIN = 0
+VMEM_MOST = 60 * 1024 * 1024
 VMEM_LIMIT = 48 * 1024 * 1024
 
 NN = (((1,), (0,)), ((), ()))
@@ -70,18 +72,45 @@
     )
 
 
-def turn_kernel(x_ref, out_ref):
-    out_ref[...] = jnp.transpose(x_ref[...])
-
-
-def pack_kernel(q_ref, k_ref, v_ref, g_ref, beta_ref, gate_ref, out_ref):
-    length, heads = beta_ref.shape
+def turn_kernel(x_ref, *out_refs):
+    first = 0
+    for out_ref in out_refs:
+        here = out_ref.shape[0]
+        out_ref[...] = jnp.transpose(x_ref[:, pl.ds(first, here)])
+        first += here
+
+
+def pack_kernel(q_ref, k_ref, v_ref, g_ref, beta_ref, gate_ref, out_ref, sems):
+    heads, length = beta_ref.shape
     width = q_ref.shape[1] // heads
-    scalars = pack_scalars(jnp.transpose(beta_ref[...]), jnp.transpose(gate_ref[...]))
+    copies = []
     for h in range(heads):
         for place, ref in enumerate((q_ref, k_ref, v_ref, g_ref)):
-            out_ref[h, pl.ds(place * length, length), :] = ref[:, pl.ds(h * width, width)]
-        out_ref[h, pl.ds(4 * length, PAD), :] = scalars[h]
+            copies.append(
+                pltpu.make_async_copy(
+                    ref.at[:, pl.ds(h * width, width)],
+                    out_ref.at[h, pl.ds(place * length, length), :],
+                    sems.at[h, place],
+                )
+            )
+            copies[-1].start()
+    for h, lines in enumerate(pack_scalars(beta_ref[...], gate_ref[...])):
+        out_ref[h, pl.ds(4 * length, PAD), :] = lines
+    for copy in copies:
+        copy.wait()
+
+
+def pack(arrays, beta, gate):
+    heads, length = beta.shape
+    width = arrays[0].shape[1] // heads
+    return pl.pallas_call(
+        pack_kernel,
+        in_specs=[pl.BlockSpec(memory_space=pl.ANY)] * 4 + [pl.BlockSpec(memory_space=pltpu.VMEM)] * 2,
+        out_specs=pl.BlockSpec(memory_space=pltpu.VMEM),
+        out_shape=jax.ShapeDtypeStruct((heads, 4 * length + PAD, width), bf16),
+        scratch_shapes=[pltpu.SemaphoreType.DMA((heads, 4))],
+        compiler_params=pltpu.CompilerParams(vmem_limit_bytes=VMEM_MOST),
+    )(*arrays, beta, gate)
 
 
 def scalars_of(slab_ref, count, length):
@@ -104,7 +133,7 @@
     return jnp.where(causal, jnp.exp(jnp.where(causal, run_col - run_row, 0.0)), 0.0)
 
 
-def first_kernel(slab_ref, maps_ref, aux_ref, ends_ref, inv_ref, low_ref):
+def first_kernel(place_ref, slab_ref, maps_ref, aux_ref, ends_ref, inv_ref, low_ref):
     count = slab_ref.shape[0]
     width = slab_ref.shape[2]
     length = (slab_ref.shape[1] - PAD) // 4
@@ -171,9 +200,10 @@
     ends_ref[0] = state
     ends_ref[1] = adjoint
     ends_ref[2] = total
-
-
-def second_kernel(slab_ref, maps_ref, aux_ref, start_ref, finish_ref, dv_ref, out_ref, state_ref, adj_ref):
+    ends_ref[3] = jnp.where(place_ref[0] == 0, state, adjoint)
+
+
+def second_kernel(place_ref, slab_ref, maps_ref, aux_ref, start_ref, finish_ref, dv_ref, out_ref, state_ref, adj_ref):
     count = slab_ref.shape[0]
     width = slab_ref.shape[2]
     length = (slab_ref.shape[1] - PAD) // 4
@@ -182,8 +212,8 @@
     causal = line >= col
     strict = line > col
 
-    state_ref[0] = start_ref[...]
-    adj_ref[count - 1] = finish_ref[...]
+    state_ref[0] = jnp.where(place_ref[0] == 0, 0.0, start_ref[...])
+    adj_ref[count - 1] = jnp.where(place_ref[0] == place_ref[1] - 1, 0.0, finish_ref[...])
     for c in range(1, count):
         state_ref[c] = mm(split(maps_ref[c - 1, 0]), split(state_ref[c - 1]), NN) + maps_ref[c - 1, 1]
         r = count - 1 - c
@@ -235,27 +265,75 @@
     return lax.ppermute(x, "seq", [(i, i ^ mask) for i in range(lax.axis_size("seq"))])
 
 
-def gather_parts(x):
-    half = x.shape[0] // 2
-    out = []
-    far = [(m, swap(x, m) if m else x) for m in range(0, lax.axis_size("seq"), 4)]
-    for m, own in far:
-        side, down = swap(own, 1), swap(own, 2)
-        out += [(m, 0, own), (m | 1, 0, side), (m | 2, 0, down)]
-        out += [(m | 3, 0, swap(down[:half], 1)), (m | 3, half, swap(side[half:], 2))]
-    return out
-
-
-def place_kernel(where, place_ref, *refs):
-    parts, (all_ref, rows_ref) = refs[: len(where)], refs[len(where) :]
-    shards, count, length, width = all_ref.shape
-    heads = rows_ref.shape[1] // width
-    me = place_ref[0]
-    for (mask, first), part in zip(where, parts):
-        all_ref[me ^ mask, pl.ds(first, part.shape[0])] = part[...]
-    group = me // heads * heads
-    for h in range(heads):
-        rows_ref[:, pl.ds(h * width, width)] = all_ref[group + h, me - group]
+def corner(got, m):
+    got[m | 3] = swap(got[m | 2], 1) if m == 12 else swap(got[m | 1], 2)
+
+
+def sides(got, m):
+    if m == 4:
+        got[5], got[6] = swap(got[1], 4), swap(got[2], 4)
+    else:
+        got[m | 1], got[m | 2] = swap(got[m], 1), swap(got[m], 2)
+
+
+def after(got, masks, *others):
+    some = {m: got[m] for m in masks}
+    return {**got, **lax.optimization_barrier((some,) + others)[0]}
+
+
+def tied(x, got, masks):
+    x, some = lax.optimization_barrier((x, {m: got[m] for m in masks if m in got}))
+    return x, {**got, **some}
+
+
+def stack_kernel(me_ref, *refs):
+    parts, out_ref, sems = refs[:-2], refs[-2], refs[-1]
+    copies = []
+    for mask, part in enumerate(parts):
+        copies.append(pltpu.make_async_copy(part, out_ref.at[me_ref[0] ^ mask], sems.at[mask]))
+        copies[-1].start()
+    for copy in copies:
+        copy.wait()
+
+
+def place_kernel(masks, all_heads, me_ref, *refs):
+    parts, all_ref, sems = refs[:-2], refs[-2], refs[-1]
+    width = parts[0].shape[2]
+    heads = all_ref.shape[3] // width
+    copies = []
+    for i, (mask, part) in enumerate(zip(masks, parts)):
+        source = me_ref[0] ^ mask
+        lanes = pl.ds(pl.multiple_of(source % heads * width, width), width)
+        copies.append(pltpu.make_async_copy(part, all_ref.at[source // all_heads, :, :, lanes], sems.at[i]))
+        copies[-1].start()
+    for copy in copies:
+        copy.wait()
+
+
+def rows_kernel(me_ref, *refs):
+    parts, rows_ref, sems = refs[:-2], refs[-2], refs[-1]
+    heads, width = len(parts), parts[0].shape[2]
+    me = me_ref[0]
+    copies = []
+    for mask, part in enumerate(parts):
+        lanes = pl.ds(pl.multiple_of((me ^ mask) % heads * width, width), width)
+        copies.append(pltpu.make_async_copy(part.at[me % heads], rows_ref.at[:, lanes], sems.at[mask]))
+        copies[-1].start()
+    for copy in copies:
+        copy.wait()
+
+
+def arranged(kernel, got, me, outs):
+    parts = [got[m] for m in sorted(got)]
+    vmem = pl.BlockSpec(memory_space=pltpu.VMEM)
+    return pl.pallas_call(
+        kernel,
+        in_specs=[pl.BlockSpec(memory_space=pltpu.SMEM)] + [pl.BlockSpec(memory_space=pl.ANY)] * len(parts),
+        out_specs=[vmem] * len(outs),
+        out_shape=[jax.ShapeDtypeStruct(o, bf16) for o in outs],
+        scratch_shapes=[pltpu.SemaphoreType.DMA((len(parts),))],
+        compiler_params=pltpu.CompilerParams(vmem_limit_bytes=VMEM_LIMIT),
+    )(me.reshape(1), *parts)
 
 
 def unpack_kernel(back_ref, dq_ref, dk_ref, dbeta_ref, dgate_ref):
@@ -269,48 +347,88 @@
         b, g = unpack_scalars(back_ref[h, pl.ds(2 * length, PAD), :])
         betas.append(b)
         gates.append(g)
-    dbeta_ref[...] = jnp.transpose(jnp.concatenate(betas, axis=0))
-    dgate_ref[...] = jnp.transpose(jnp.concatenate(gates, axis=0))
-
-
-def weight_kernel(x_ref, dv_ref, out_ref):
-    shards = x_ref.shape[0]
-    groups, heads, count = dv_ref.shape[:3]
-    total = None
-    step = 2 if count % 2 == 0 else 1
-    for s in range(0, shards, step):
-        left = join([x_ref[s + i, 0] for i in range(step)], 1)
-        right = join(
-            [join([dv_ref[(s + i) // count, h, (s + i) % count] for h in range(heads)], 1) for i in range(step)], 0
-        )
-        term = dot(left, right, NN)
-        total = term if total is None else total + term
-    out_ref[...] = total.astype(out_ref.dtype)
-
-
-def weight_grad(x_all, dv_all, block):
-    shards, halves, feats, length = x_all.shape
-    groups, heads, count, _, width = dv_all.shape
-    per = feats // block
+    dbeta_ref[...] = jnp.concatenate(betas, axis=0)
+    dgate_ref[...] = jnp.concatenate(gates, axis=0)
+
+
+def weight_kernel(starts, place_ref, *refs):
+    x_refs, right_ref, out_ref = refs[: len(starts) - 1], refs[len(starts) - 1], refs[-1]
+    step = pl.program_id(0)
+    for ref, first, last in zip(x_refs, starts, starts[1:]):
+
+        @pl.when((step >= first) & (step < last))
+        def _():
+            left = [ref[j, 0] for j in range(ref.shape[0])]
+            out_ref[...] = dot(join(left, 1), right_ref[...], NN).astype(out_ref.dtype)
+
+
+def weight_grad(plain, rest, right, where, blocks, before):
+    shards, length = (rest[0] if plain is None else plain).shape[0 :: 2 if plain is None else 3]
+    bands = lax.axis_size("head")
+    cut = 0 if plain is None else plain.shape[2]
+    left_over = rest[0].shape[1] if rest else 0
+    block = 1024
+    while cut % block or left_over % block or shards * block * length * 4 * (len(rest) + 1) > 2**25:
+        block = block // 2
+    per, more = cut // block, left_over // block
+    total = per + more
+    arrays, starts, specs = [], [0], []
+
+    def add(x, steps):
+        begin = starts[-1]
+        arrays.append(x)
+        starts.append(begin + steps)
+        inner = x.shape[2] // block
+
+        def index(t, p):
+            at = jnp.clip(t - begin, 0, steps - 1)
+            return (0, at // inner, at % inner, 0)
+
+        specs.append(pl.BlockSpec((shards, 1, block, length), index))
+
+    if cut:
+        add(plain, bands * per)
+    for x in rest:
+        add(x[:, None], more)
+
+    def out_index(t, p):
+        place = (t // max(per, 1)) * total + t % max(per, 1)
+        for r in range(len(rest)):
+            at = t - bands * per - r * more
+            band = (p[0] + bands - r) % bands
+            place = jnp.where(at >= 0, band * total + per + at, place)
+        return (place, p[1])
+
+    extra = [] if before is None else [before]
     return pl.pallas_call(
-        weight_kernel,
-        grid=(halves * per,),
-        in_specs=[
-            pl.BlockSpec((shards, 1, block, length), lambda i: (0, i // per, i % per, 0)),
-            pl.BlockSpec(dv_all.shape, lambda i: (0, 0, 0, 0, 0)),
-        ],
-        out_specs=pl.BlockSpec((block, heads * width), lambda i: (i, 0)),
-        out_shape=jax.ShapeDtypeStruct((halves * feats, heads * width), bf16),
+        partial(weight_kernel, starts),
+        grid_spec=pltpu.PrefetchScalarGridSpec(
+            num_scalar_prefetch=1,
+            grid=(starts[-1],),
+            in_specs=specs
+            + [pl.BlockSpec(right.shape, lambda t, p: (0, 0))]
+            + [pl.BlockSpec(memory_space=pl.ANY)] * len(extra),
+            out_specs=pl.BlockSpec((block, right.shape[1]), out_index),
+        ),
+        out_shape=jax.ShapeDtypeStruct((bands * total * block, right.shape[1] * blocks), bf16),
+        input_output_aliases={len(arrays) + 2: 0} if extra else {},
         compiler_params=pltpu.CompilerParams(vmem_limit_bytes=VMEM_LIMIT),
-    )(x_all, dv_all)
-
-
-def whole_call(kernel, outs, scratch=(), flops=0):
+        cost_estimate=pl.CostEstimate(flops=10**10, bytes_accessed=0, transcendentals=0),
+    )(where, *arrays, right, *extra)
+
+
+def whole_call(kernel, outs, scratch=(), flops=0, scalars=0):
+    specs = {}
+    if scalars:
+        vmem = pl.BlockSpec(memory_space=pltpu.VMEM)
+        specs = dict(in_specs=[pl.BlockSpec(memory_space=pltpu.SMEM)] + [vmem] * scalars)
     return pl.pallas_call(
         kernel,
+        **specs,
         out_shape=[jax.ShapeDtypeStruct(s, d) for s, d in outs],
         scratch_shapes=[pltpu.VMEM(s, d) for s, d in scratch],
         compiler_params=pltpu.CompilerParams(vmem_limit_bytes=VMEM_LIMIT),
+        cost_estimate=pl.CostEstimate(flops=int(flops), bytes_accessed=0, transcendentals=0),
     )
 
 
@@ -322,61 +440,122 @@
     groups = seq // heads
     count = heads
     members = [[g * heads + i for i in range(heads)] for g in range(groups)]
-
-    slabs = whole_call(pack_kernel, [((heads, 4 * length + PAD, width), bf16)])(
-        query_rows, key_matrix_rows, value_rows, grad_out, beta_rows, log_gate
-    )[0]
+    far = list(range(4, seq, 4))
+    beyond = [m for m in far if m not in (4, 8)]
+    me = lax.axis_index("seq").astype(jnp.int32)
+    core = lax.axis_index("head").astype(jnp.int32)
+    place = jnp.stack([me // heads, jnp.int32(groups)])
+
+    feats = layer_input.shape[1]
+    cut = feats * PLAIN // 8
+    sizes = [size for size in (cut, feats - cut) if size]
+    turned = whole_call(turn_kernel, [((size, length), bf16) for size in sizes])(layer_input)
+    plain = None
+    if cut:
+        plain = lax.all_gather(turned[0], ("seq", "head"), axis=0).reshape(seq, halves, cut, length)
+    got = {0: turned[-1]}
+    for m in beyond + [1, 2]:
+        got[m] = swap(got[0], m)
+
+    slabs = pack([query_rows, key_matrix_rows, value_rows, grad_out], beta_rows.T, log_gate.T)
     slabs = lax.all_to_all(slabs, "seq", 0, 0, axis_index_groups=members, tiled=True)
-    turned = whole_call(turn_kernel, [(layer_input.shape[::-1], bf16)])(layer_input)[0]
-    x_all = lax.all_gather(turned, ("seq", "head"), axis=0).reshape(
-        (seq, halves) + turned.shape
-    )
+    for m in far[:1]:
+        got[m] = swap(got[0], m)
 
     square = (width, width)
     maps, aux, ends = whole_call(
         first_kernel,
-        [((count, 3) + square, f32), ((count, 4, length, width), f32), ((3,) + square, f32)],
+        [((count, 3) + square, f32), ((count, 4, length, width), f32), ((4,) + square, f32)],
         [((count, length, length), f32), ((count, length, length), f32)],
-    )(slabs)
+        9e9,
+        1,
+    )(place, slabs)
+
+    got = after(got, list(got), ends)
+    corner(got, 0)
+    if 12 in got:
+        got[8] = swap(got[12], 4)
+    for m in beyond:
+        sides(got, m)
+
     up = [(s, s + heads) for s in range(seq - heads)]
     down = [(s + heads, s) for s in range(seq - heads)]
-    start = lax.ppermute(ends[0], "seq", up)
-    finish = lax.ppermute(ends[1], "seq", down)
-    for _ in range(groups - 2):
-        start = lax.ppermute(
-            jnp.matmul(ends[2], start, precision=lax.Precision.HIGHEST) + ends[0], "seq", up
-        )
-        finish = lax.ppermute(
-            jnp.matmul(finish, ends[2], precision=lax.Precision.HIGHEST) + ends[1], "seq", down
-        )
+    if groups == 2:
+        start = finish = lax.ppermute(ends[3], "seq", up + down)
+    else:
+        start = lax.ppermute(ends[0], "seq", up)
+        finish = lax.ppermute(ends[1], "seq", down)
+        for _ in range(groups - 2):
+            start = lax.ppermute(
+                jnp.matmul(ends[2], start, precision=lax.Precision.HIGHEST) + ends[0], "seq", up
+            )
+            finish = lax.ppermute(
+                jnp.matmul(finish, ends[2], precision=lax.Precision.HIGHEST) + ends[1], "seq", down
+            )
+
+    if groups == 2:
+        start, got = tied(start, got, [3, 4, 8, 13, 14])
+        finish = start
+    for m in far[:2]:
+        sides(got, m)
+    for m in beyond:
+        corner(got, m)
 
     dv, grads = whole_call(
         second_kernel,
         [((count, length, width), bf16), ((count, 2 * length + PAD, width), bf16)],
         [((count,) + square, f32), ((count,) + square, f32)],
-    )(slabs, maps, aux, start, finish)
+        7e9,
+        5,
+    )(place, slabs, maps, aux, start, finish)
+
+    dv, got = tied(dv, got, [m for m in (9, 10) if m in got])
+    sent = {0: dv}
+    for m in beyond[1:] + far[1:2] + [1, 2]:
+        sent[m] = swap(dv, m)
+    for m in far[:2]:
+        corner(got, m)
+    sent, got = lax.optimization_barrier((sent, got))
+    for m in far[1:2]:
+        sides(sent, m)
+    for m in far[:1]:
+        sent[m] = swap(dv, m)
+    if 8 in sent:
+        sent[12] = swap(sent[8], 4)
+    sent[3] = swap(sent[2], 1)
+    (own,) = arranged(stack_kernel, got, me, [(seq,) + got[0].shape])
+    own, sent = tied(own, sent, list(sent))
+    rest = [own]
+    for r in range(1, halves):
+        rest.append(lax.ppermute(own, "head", [(i, (i + r) % halves) for i in range(halves)]))
+    for m in far[1:2]:
+        sent[m | 3] = swap(sent[m | 1], 2)
+    for m in far[:1] + beyond:
+        sides(sent, m)
+
+    sent = after(sent, [m for m in sent if m % 8 > 3], sent[11 if 8 in sent else 3])
+    for m in far[:1] + beyond:
+        corner(sent, m)
+
+    rows = (length, heads * width)
+    (dvo,) = arranged(rows_kernel, {m: sent[m] for m in range(heads)}, me, [rows])
+    weight = None
+    part = max(heads // 2, 1)
+    for bit in sorted({0, part % heads}):
+        some = {m: sent[m] for m in range(seq) if m & part == bit or heads == 1}
+        if weight is not None:
+            some = after(some, list(some), weight)
+        (right,) = arranged(partial(place_kernel, list(some), heads), some, me, [(groups, count, length, part * width)])
+        where = jnp.stack([core, (me % heads ^ bit) // part])
+        weight = weight_grad(plain, rest, right.reshape(seq * length, part * width), where, heads // part, weight)
+
     back = lax.all_to_all(grads, "seq", 0, 0, axis_index_groups=members, tiled=True)
-
     rows = (length, heads * width)
-    parts = gather_parts(dv)
-    me = lax.axis_index("seq").astype(jnp.int32).reshape(1)
-    vmem = pl.BlockSpec(memory_space=pltpu.VMEM)
-    dv_all, dvo = pl.pallas_call(
-        partial(place_kernel, [p[:2] for p in parts]),
-        in_specs=[pl.BlockSpec(memory_space=pltpu.SMEM)] + [vmem] * len(parts),
-        out_specs=[vmem, vmem],
-        out_shape=[
-            jax.ShapeDtypeStruct((seq, count, length, width), bf16),
-            jax.ShapeDtypeStruct(rows, bf16),
-        ],
-        compiler_params=pltpu.CompilerParams(vmem_limit_bytes=VMEM_LIMIT),
-    )(me, *[p[2] for p in parts])
-    dv_all = dv_all.reshape(groups, heads, count, length, width)
+    back = lax.optimization_barrier((back, weight))[0]
     dq, dk, dbeta, dgate = whole_call(
-        unpack_kernel, [(rows, bf16), (rows, bf16), ((length, heads), f32), ((length, heads), f32)]
+        unpack_kernel, [(rows, bf16), (rows, bf16), ((heads, length), f32), ((heads, length), f32)]
     )(back)
-    weight = weight_grad(x_all, dv_all, min(512, layer_input.shape[1]))
-    return dq, dk, dvo, dbeta, dgate, weight
+    return dq, dk, dvo, dbeta.T, dgate.T, weight
 
 
 def solution(mesh):

time: 196 us -> 181 us (0.923)
  blocking collectives: 32.9 us -> 0 us
  starting transfers between devices: 33.1 us -> 60 us
  Pallas kernels: 43 us -> 58.4 us
  local copies, waits for them, and re-layouts: 19 us -> 4.98 us
  between operations: 14.1 us -> 0.84 us
  waiting for transfers between devices: 53.7 us -> 55.9 us
    all_to_all x1 -> x0, blocking collectives: 32.9 us -> none  [shards(): lax.all_to_all(slabs, 'seq', 0, 0, axis_index_groups=members, tiled=True)]
    ppermute x19 -> x30, starting transfers between devices: 22.6 us -> 39.9 us  [swap(): lax.ppermute(x, 'seq', [(i, i ^ mask) for i in range(lax.axis_size('seq'))])]
    pallas_call x5 -> x9, Pallas kernels: 27.1 us -> 41.2 us  [the longest x2 29.5 us: weight_grad(): pl.pallas_call(partial(weight_kernel, starts), grid_spec=pltpu.PrefetchSc...]
    unnamed x32 -> x26, local copies, waits for them, and re-layouts: 15.6 us -> 4.98 us
    all_to_all x0 -> x1, waiting for transfers between devices: none -> 8.91 us  [shards(): lax.all_to_all(slabs, 'seq', 0, 0, axis_index_groups=members, tiled=True)]
    all_to_all x0 -> x1, starting transfers between devices: none -> 6.2 us  [shards(): lax.all_to_all(slabs, 'seq', 0, 0, axis_index_groups=members, tiled=True)]
    ppermute x2, waiting for transfers between devices: 4.29 us -> 0.01 us  [the longest x1 0.01 us: shards(): start = finish = lax.ppermute(ends[3], 'seq', up + down)]
    ppermute x2, starting transfers between devices: 6.92 us -> 10.3 us  [the longest x1 10.3 us: shards(): start = finish = lax.ppermute(ends[3], 'seq', up + down)]
  transfers between devices with their start and end apart: 23 -> 34, of which waited for: 10 -> 12; matrix products, arithmetic and copies ran while one was open for 3% -> 0% of each run, Pallas kernels for 11% -> 30%
where the time goes in v2:
time: 181 us; the launch traced here: 180 us
  starting transfers between devices  60 us (33%)
  Pallas kernels  58.4 us (32%)
  waiting for transfers between devices  55.9 us (31%)
  local copies, waits for them, and re-layouts  4.98 us (3%)
    ppermute x30, waiting for transfers between devices, swap(): lax.ppermute(x, 'seq', [(i, i ^ mask) for i in range(lax.axis_size('seq'))])  47 us
    ppermute x30, starting transfers between devices, swap(): lax.ppermute(x, 'seq', [(i, i ^ mask) for i in range(lax.axis_size('seq'))])  39.9 us
    pallas_call x2, Pallas kernels, weight_grad(): pl.pallas_call(partial(weight_kernel, starts), grid_spec=pltpu.PrefetchSc...  29.5 us
    ppermute x1, starting transfers between devices, shards(): start = finish = lax.ppermute(ends[3], 'seq', up + down)  10.3 us
    pallas_call x1, Pallas kernels, shards(): whole_call(first_kernel, [((count, 3) + square, f32), ((count, 4, length,...  9.65 us
    all_to_all x1, waiting for transfers between devices, shards(): lax.all_to_all(slabs, 'seq', 0, 0, axis_index_groups=members, tiled=True)  8.91 us
    pallas_call x1, Pallas kernels, shards(): whole_call(second_kernel, [((count, length, width), bf16), ((count, 2 * l...  7.59 us
    pallas_call x4, Pallas kernels, arranged(): pl.pallas_call(kernel, in_specs=[pl.BlockSpec(memory_space=pltpu.SMEM)] +...  7.37 us
  transfers between devices with their start and end apart: 34, of which 12 were waited for; matrix products, arithmetic and copies ran while one was open for 0% of the time, Pallas kernels for 30%

profile of v2, /device:TPU:0, one launch (start us, length us, event | category | flops | bytes accessed | tf_op | source)
XLA Modules:
  0.0 180.4 jit_solution(12287711655478846647)
XLA Ops:
  0.6 3.2 %shard_map.118 = bf16[8,528,128]{2,1,0:T(8,128)(2,1)} custom-call(bf16[128,1024]{1,0:T(8,128)(2,1)} %q_ref.1, bf16[128,1024]{1,0:T(8,128)(2,1)} %k_ref.1, bf16[128,1024]{1,0:T(8,128)(2,1)} %v_ref.1, bf16[128,1024]{1,0:T(8,128)(2,1)} %g_ref.1, f32[8,128]{1,0:T(8,128)} %bitcast.19, f32[8,128]{1,0:T(8,128)} %bitcast.20), custom_call_target="tpu_custom_call" | custom-call | tf_op jit(solution)/shard_map/pallas_call | solution.py:106
  3.9 6.2 %all-to-all-start = ((bf16[8,528,128]{2,1,0:T(8,128)(2,1)}), bf16[8,528,128]{2,1,0:T(8,128)(2,1)S(1)}, u32[]{:S(2)}, u32[]{:S(2)}) async-start(bf16[8,528,128]{2,1,0:T(8,128)(2,1)} %shard_map.118), calls=%async_computation | async-start | bytes 2162688 | tf_op jit(solution)/shard_map/all_to_all | solution.py:461
  10.3 4.1 %collective-permute-start.4 = (bf16[2048,128]{1,0:T(8,128)(2,1)S(1)}, bf16[2048,128]{1,0:T(8,128)(2,1)}, u32[]{:S(2)}, u32[]{:S(2)}) collective-permute-start(bf16[2048,128]{1,0:T(8,128)(2,1)S(1)} %shard_map.120.refs_0_), channel_id=1, source_target_pairs={{0,24},{2,26},{4,28},{6,30},{8,16},{10,18},{12,20},{14,22},{16,8},... | collective-permute-start | bytes 1572872 | tf_op jit(solution)/shard_map/ppermute | solution.py:265
  14.4 1.5 collective-permute-start.2
  17.4 8.9 %all-to-all-done.slab_ref = bf16[8,528,128]{2,1,0:T(8,128)(2,1)S(1)} async-done(((bf16[8,528,128]{2,1,0:T(8,128)(2,1)}), bf16[8,528,128]{2,1,0:T(8,128)(2,1)S(1)}, u32[]{:S(2)}, u32[]{:S(2)}) %all-to-all-start) | async-done | bytes 1081376 | tf_op jit(solution)/shard_map/all_to_all | solution.py:461
  26.3 9.7 %shard_map.119 = (f32[8,3,128,128]{3,2,1,0:T(8,128)S(1)}, f32[8,4,128,128]{3,2,1,0:T(8,128)S(1)}, f32[4,128,128]{2,1,0:T(8,128)S(1)}) custom-call(s32[2]{0:T(128)S(1)} %pad_add_fusion.place_ref, bf16[8,528,128]{2,1,0:T(8,128)(2,1)S(1)} %all-to-all-done.slab_ref), custom_call_target="tpu_custom_call" | custom-call | flops 8999999488 | tf_op jit(solution)/shard_map/pallas_call | solution.py:466
  36.0 10.3 %collective-permute-start = (f32[128,128]{1,0:T(8,128)S(1)}, f32[128,128]{1,0:T(8,128)S(1)}, u32[]{:S(2)}, u32[]{:S(2)}) collective-permute-start(f32[128,128]{1,0:T(8,128)S(1)} %slice_bitcast_fusion), channel_id=1, source_target_pairs={{0,16},{2,18},{4,20},{6,22},{8,24},{10,26},{12,28},{14,30},{16,0},... | collective-permute-start | bytes 196616 | tf_op jit(solution)/shard_map/ppermute | solution.py:484
  47.2 1.5 collective-permute-start.5
  50.7 2.4 %collective-permute-start.6 = (bf16[2048,128]{1,0:T(8,128)(2,1)}, bf16[2048,128]{1,0:T(8,128)(2,1)S(1)}, u32[]{:S(2)}, u32[]{:S(2)}) collective-permute-start(bf16[2048,128]{1,0:T(8,128)(2,1)} %collective-permute-done.4.refs_12_), channel_id=1, source_target_pairs={{0,8},{2,10},{4,12},{6,14},{8,0},{10,2},{12,4},{14,6},{16,24},{18,... | collective-permute-start | bytes 1572872 | tf_op jit(solution)/shard_map/ppermute | solution.py:265
  53.2 8.9 %collective-permute-done.5.refs_3_ = bf16[2048,128]{1,0:T(8,128)(2,1)S(1)} collective-permute-done((bf16[2048,128]{1,0:T(8,128)(2,1)S(1)}, bf16[2048,128]{1,0:T(8,128)(2,1)S(1)}, u32[]{:S(2)}, u32[]{:S(2)}) %collective-permute-start.5) | collective-permute-done | bytes 524320 | tf_op jit(solution)/shard_map/ppermute | solution.py:265
  62.1 1.9 %collective-permute-start.15 = (bf16[2048,128]{1,0:T(8,128)(2,1)S(1)}, bf16[2048,128]{1,0:T(8,128)(2,1)S(1)}, u32[]{:S(2)}, u32[]{:S(2)}) collective-permute-start(bf16[2048,128]{1,0:T(8,128)(2,1)S(1)} %collective-permute-done.2.refs_2_), channel_id=1, source_target_pairs={{0,8},{2,10},{4,12},{6,14},{8,0},{10,2},{12,4},{14,6},{16,24},{18,... | collective-permute-start | bytes 1572872 | tf_op jit(solution)/shard_map/ppermute | solution.py:265
  64.0 7.0 %collective-permute-done.8.refs_14_ = bf16[2048,128]{1,0:T(8,128)(2,1)S(1)} collective-permute-done((bf16[2048,128]{1,0:T(8,128)(2,1)}, bf16[2048,128]{1,0:T(8,128)(2,1)S(1)}, u32[]{:S(2)}, u32[]{:S(2)}) %collective-permute-start.8) | collective-permute-done | bytes 524320 | tf_op jit(solution)/shard_map/ppermute | solution.py:265
  71.0 1.5 collective-permute-start.10
  74.6 2.9 %collective-permute-done.14.refs_5_ = bf16[2048,128]{1,0:T(8,128)(2,1)S(1)} collective-permute-done((bf16[2048,128]{1,0:T(8,128)(2,1)S(1)}, bf16[2048,128]{1,0:T(8,128)(2,1)S(1)}, u32[]{:S(2)}, u32[]{:S(2)}) %collective-permute-start.14) | collective-permute-done | bytes 524320 | tf_op jit(solution)/shard_map/ppermute | solution.py:265
  77.5 1.5 collective-permute-start.16
  78.9 7.6 %shard_map.121 = (bf16[8,128,128]{2,1,0:T(8,128)(2,1)S(1)}, bf16[8,272,128]{2,1,0:T(8,128)(2,1)}) custom-call(s32[2]{0:T(128)S(1)} %pad_add_fusion.place_ref, bf16[8,528,128]{2,1,0:T(8,128)(2,1)S(1)} %all-to-all-done.slab_ref, f32[8,3,128,128]{3,2,1,0:T(8,128)S(1)} %get-tuple-element.74.maps_ref, f32[8,4,128,128]{3,2,1,0:T(8,128)S(1)} %get-tuple-element.75.aux_ref, ...), custom_call_target="tpu_custom_call" | custom-call | flops 7000000000 | tf_op jit(solution)/shard_map/pallas_call | solution.py:504
  87.9 2.1 %collective-permute-start.13 = (bf16[8,128,128]{2,1,0:T(8,128)(2,1)S(1)}, bf16[8,128,128]{2,1,0:T(8,128)(2,1)S(1)}, u32[]{:S(2)}, u32[]{:S(2)}) collective-permute-start(bf16[8,128,128]{2,1,0:T(8,128)(2,1)S(1)} %get-tuple-element.125.refs_0_), channel_id=1, source_target_pairs={{0,16},{2,18},{4,20},{6,22},{8,24},{10,26},{12,28},{14,30},{16,0},... | collective-permute-start | bytes 786440 | tf_op jit(solution)/shard_map/ppermute | solution.py:265
  90.0 1.5 collective-permute-start.12
  91.5 5.7 %collective-permute-done.16.refs_7_ = bf16[2048,128]{1,0:T(8,128)(2,1)S(1)} collective-permute-done((bf16[2048,128]{1,0:T(8,128)(2,1)S(1)}, bf16[2048,128]{1,0:T(8,128)(2,1)S(1)}, u32[]{:S(2)}, u32[]{:S(2)}) %collective-permute-start.16) | collective-permute-done | bytes 524320 | tf_op jit(solution)/shard_map/ppermute | solution.py:265
  98.6 1.9 %collective-permute-start.20 = (bf16[8,128,128]{2,1,0:T(8,128)(2,1)S(1)}, bf16[8,128,128]{2,1,0:T(8,128)(2,1)S(1)}, u32[]{:S(2)}, u32[]{:S(2)}) collective-permute-start(bf16[8,128,128]{2,1,0:T(8,128)(2,1)S(1)} %get-tuple-element.125.refs_0_), channel_id=1, source_target_pairs={{0,8},{2,10},{4,12},{6,14},{8,0},{10,2},{12,4},{14,6},{16,24},{18,... | collective-permute-start | bytes 786440 | tf_op jit(solution)/shard_map/ppermute | solution.py:265
  100.6 10.2 %collective-permute-done.12.refs_2_ = bf16[8,128,128]{2,1,0:T(8,128)(2,1)S(1)} collective-permute-done((bf16[8,128,128]{2,1,0:T(8,128)(2,1)S(1)}, bf16[8,128,128]{2,1,0:T(8,128)(2,1)S(1)}, u32[]{:S(2)}, u32[]{:S(2)}) %collective-permute-start.12) | collective-permute-done | bytes 262176 | tf_op jit(solution)/shard_map/ppermute | solution.py:265
  110.8 1.7 collective-permute-start.19
  114.3 5.5 %shard_map.122 = bf16[16,2048,128]{2,1,0:T(8,128)(2,1)} custom-call(s32[1]{0:T(128)} %bitcast.6.me_ref, bf16[2048,128]{1,0:T(8,128)(2,1)S(1)} %shard_map.120.refs_0_, bf16[2048,128]{1,0:T(8,128)(2,1)S(1)} %collective-permute-done.1.refs_1_, bf16[2048,128]{1,0:T(8,128)(2,1)S(1)} %collective-permute-done.2.refs_2_, ...), custom_call_target="tpu_custom_call" | custom-call | tf_op jit(solution)/shard_map/pallas_call | solution.py:329
  121.5 1.5 collective-permute-start.29
  124.1 1.6 collective-permute-start.26
  126.3 4.3 %collective-permute-done.29.refs_7_ = bf16[8,128,128]{2,1,0:T(8,128)(2,1)S(1)} collective-permute-done((bf16[8,128,128]{2,1,0:T(8,128)(2,1)S(1)}, bf16[8,128,128]{2,1,0:T(8,128)(2,1)S(1)}, u32[]{:S(2)}, u32[]{:S(2)}) %collective-permute-start.29) | collective-permute-done | bytes 262176 | tf_op jit(solution)/shard_map/ppermute | solution.py:265
  132.8 4.9 %collective-permute-done.26.refs_2_.refs_6_ = bf16[8,128,128]{2,1,0:T(8,128)(2,1)S(1)} collective-permute-done((bf16[8,128,128]{2,1,0:T(8,128)(2,1)S(1)}, bf16[8,128,128]{2,1,0:T(8,128)(2,1)S(1)}, u32[]{:S(2)}, u32[]{:S(2)}) %collective-permute-start.26) | collective-permute-done | bytes 262176 | tf_op jit(solution)/shard_map/ppermute | solution.py:265
  138.2 1.5 collective-permute-start.30
  139.8 3.5 %all-to-all-start.1 = ((bf16[8,272,128]{2,1,0:T(8,128)(2,1)}), bf16[8,272,128]{2,1,0:T(8,128)(2,1)S(1)}, u32[]{:S(2)}, u32[]{:S(2)}) async-start(bf16[8,272,128]{2,1,0:T(8,128)(2,1)} %get-tuple-element.81), calls=%async_computation.1 | async-start | bytes 1114112 | tf_op jit(solution)/shard_map/all_to_all | solution.py:552
  143.3 1.9 %collective-permute-start.31 = (bf16[8,128,128]{2,1,0:T(8,128)(2,1)S(1)}, bf16[8,128,128]{2,1,0:T(8,128)(2,1)S(1)}, u32[]{:S(2)}, u32[]{:S(2)}) collective-permute-start(bf16[8,128,128]{2,1,0:T(8,128)(2,1)S(1)} %collective-permute-done.28.refs_6_), channel_id=1, source_target_pairs={{0,2},{2,0},{4,6},{6,4},{8,10},{10,8},{12,14},{14,12},{16,18},{18,... | collective-permute-start | bytes 786440 | tf_op jit(solution)/shard_map/ppermute | solution.py:265
  149.5 14.7 %shard_map.124.refs_3_ = bf16[4096,1024]{1,0:T(8,128)(2,1)} custom-call(s32[2]{0:T(128)S(1)} %pad_add_fusion.2.place_ref, bf16[16,1,2048,128]{3,2,1,0:T(8,128)(2,1)} %bitcast.17, bf16[16,1,2048,128]{3,2,1,0:T(8,128)(2,1)} %bitcast.8.refs_1_, bf16[2048,512]{1,0:T(8,128)(2,1)S(1)} %bitcast.15), custom_call_target="tpu_custom_call" | custom-call | flops 10000000000 | tf_op jit(solution)/shard_map/pallas_call | solution.py:403
  164.7 14.7 %shard_map.126 = bf16[4096,1024]{1,0:T(8,128)(2,1)} custom-call(s32[2]{0:T(128)S(1)} %pad_add_fusion.1.place_ref, bf16[16,1,2048,128]{3,2,1,0:T(8,128)(2,1)} %bitcast.18, bf16[16,1,2048,128]{3,2,1,0:T(8,128)(2,1)} %bitcast.8.refs_1_, bf16[2048,512]{1,0:T(8,128)(2,1)S(1)} %bitcast.16, ...), custom_call_target="tpu_custom_call", output_to_operand_aliasing={{}: (4, {})} | custom-call | flops 10000000000 | tf_op jit(solution)/shard_map/pallas_call | solution.py:403
  (77 shorter events, 23.2 us)
Async XLA Ops:
  3.9 22.4 %all-to-all-start = ((bf16[8,528,128]{2,1,0:T(8,128)(2,1)}), bf16[8,528,128]{2,1,0:T(8,128)(2,1)S(1)}, u32[]{:S(2)}, u32[]{:S(2)}) async-start(bf16[8,528,128]{2,1,0:T(8,128)(2,1)} %shard_map.118), calls=%async_computation | async-start | bytes 2162688 | tf_op jit(solution)/shard_map/all_to_all | solution.py:461
  10.3 36.0 %collective-permute-start.4 = (bf16[2048,128]{1,0:T(8,128)(2,1)S(1)}, bf16[2048,128]{1,0:T(8,128)(2,1)}, u32[]{:S(2)}, u32[]{:S(2)}) collective-permute-start(bf16[2048,128]{1,0:T(8,128)(2,1)S(1)} %shard_map.120.refs_0_), channel_id=1, source_target_pairs={{0,24},{2,26},{4,28},{6,30},{8,16},{10,18},{12,20},{14,22},{16,8},... | collective-permute-start | bytes 1572872 | tf_op jit(solution)/shard_map/ppermute | solution.py:265
  14.4 32.9 %collective-permute-start.3 = (bf16[2048,128]{1,0:T(8,128)(2,1)S(1)}, bf16[2048,128]{1,0:T(8,128)(2,1)S(1)}, u32[]{:S(2)}, u32[]{:S(2)}) collective-permute-start(bf16[2048,128]{1,0:T(8,128)(2,1)S(1)} %shard_map.120.refs_0_), channel_id=1, source_target_pairs={{0,8},{2,10},{4,12},{6,14},{8,0},{10,2},{12,4},{14,6},{16,24},{18,... | collective-permute-start | bytes 1572872 | tf_op jit(solution)/shard_map/ppermute | solution.py:265
  14.4 32.9 %collective-permute-start.2 = (bf16[2048,128]{1,0:T(8,128)(2,1)S(1)}, bf16[2048,128]{1,0:T(8,128)(2,1)S(1)}, u32[]{:S(2)}, u32[]{:S(2)}) collective-permute-start(bf16[2048,128]{1,0:T(8,128)(2,1)S(1)} %shard_map.120.refs_0_), channel_id=1, source_target_pairs={{0,4},{2,6},{4,0},{6,2},{8,12},{10,14},{12,8},{14,10},{16,20},{18,... | collective-permute-start | bytes 1572872 | tf_op jit(solution)/shard_map/ppermute | solution.py:265
  15.8 31.4 %collective-permute-start.1 = (bf16[2048,128]{1,0:T(8,128)(2,1)S(1)}, bf16[2048,128]{1,0:T(8,128)(2,1)S(1)}, u32[]{:S(2)}, u32[]{:S(2)}) collective-permute-start(bf16[2048,128]{1,0:T(8,128)(2,1)S(1)} %shard_map.120.refs_0_), channel_id=1, source_target_pairs={{0,2},{2,0},{4,6},{6,4},{8,10},{10,8},{12,14},{14,12},{16,18},{18,... | collective-permute-start | bytes 1572872 | tf_op jit(solution)/shard_map/ppermute | solution.py:265
  36.0 17.2 %collective-permute-start = (f32[128,128]{1,0:T(8,128)S(1)}, f32[128,128]{1,0:T(8,128)S(1)}, u32[]{:S(2)}, u32[]{:S(2)}) collective-permute-start(f32[128,128]{1,0:T(8,128)S(1)} %slice_bitcast_fusion), channel_id=1, source_target_pairs={{0,16},{2,18},{4,20},{6,22},{8,24},{10,26},{12,28},{14,30},{16,0},... | collective-permute-start | bytes 196616 | tf_op jit(solution)/shard_map/ppermute | solution.py:484
  47.2 14.9 %collective-permute-start.5 = (bf16[2048,128]{1,0:T(8,128)(2,1)S(1)}, bf16[2048,128]{1,0:T(8,128)(2,1)S(1)}, u32[]{:S(2)}, u32[]{:S(2)}) collective-permute-start(bf16[2048,128]{1,0:T(8,128)(2,1)S(1)} %collective-permute-done.1.refs_1_), channel_id=1, source_target_pairs={{0,4},{2,6},{4,0},{6,2},{8,12},{10,14},{12,8},{14,10},{16,20},{18,... | collective-permute-start | bytes 1572872 | tf_op jit(solution)/shard_map/ppermute | solution.py:265
  48.7 22.3 %collective-permute-start.8 = (bf16[2048,128]{1,0:T(8,128)(2,1)}, bf16[2048,128]{1,0:T(8,128)(2,1)S(1)}, u32[]{:S(2)}, u32[]{:S(2)}) collective-permute-start(bf16[2048,128]{1,0:T(8,128)(2,1)} %collective-permute-done.4.refs_12_), channel_id=1, source_target_pairs={{0,4},{2,6},{4,0},{6,2},{8,12},{10,14},{12,8},{14,10},{16,20},{18,... | collective-permute-start | bytes 1572872 | tf_op jit(solution)/shard_map/ppermute | solution.py:265
  49.3 21.7 %collective-permute-start.7 = (bf16[2048,128]{1,0:T(8,128)(2,1)}, bf16[2048,128]{1,0:T(8,128)(2,1)S(1)}, u32[]{:S(2)}, u32[]{:S(2)}) collective-permute-start(bf16[2048,128]{1,0:T(8,128)(2,1)} %collective-permute-done.4.refs_12_), channel_id=1, source_target_pairs={{0,2},{2,0},{4,6},{6,4},{8,10},{10,8},{12,14},{14,12},{16,18},{18,... | collective-permute-start | bytes 1572872 | tf_op jit(solution)/shard_map/ppermute | solution.py:265
  50.7 20.3 %collective-permute-start.6 = (bf16[2048,128]{1,0:T(8,128)(2,1)}, bf16[2048,128]{1,0:T(8,128)(2,1)S(1)}, u32[]{:S(2)}, u32[]{:S(2)}) collective-permute-start(bf16[2048,128]{1,0:T(8,128)(2,1)} %collective-permute-done.4.refs_12_), channel_id=1, source_target_pairs={{0,8},{2,10},{4,12},{6,14},{8,0},{10,2},{12,4},{14,6},{16,24},{18,... | collective-permute-start | bytes 1572872 | tf_op jit(solution)/shard_map/ppermute | solution.py:265
  53.2 24.3 %collective-permute-start.14 = (bf16[2048,128]{1,0:T(8,128)(2,1)S(1)}, bf16[2048,128]{1,0:T(8,128)(2,1)S(1)}, u32[]{:S(2)}, u32[]{:S(2)}) collective-permute-start(bf16[2048,128]{1,0:T(8,128)(2,1)S(1)} %collective-permute-done.1.refs_1_), channel_id=1, source_target_pairs={{0,8},{2,10},{4,12},{6,14},{8,0},{10,2},{12,4},{14,6},{16,24},{18,... | collective-permute-start | bytes 1572872 | tf_op jit(solution)/shard_map/ppermute | solution.py:265
  62.1 27.9 %collective-permute-start.15 = (bf16[2048,128]{1,0:T(8,128)(2,1)S(1)}, bf16[2048,128]{1,0:T(8,128)(2,1)S(1)}, u32[]{:S(2)}, u32[]{:S(2)}) collective-permute-start(bf16[2048,128]{1,0:T(8,128)(2,1)S(1)} %collective-permute-done.2.refs_2_), channel_id=1, source_target_pairs={{0,8},{2,10},{4,12},{6,14},{8,0},{10,2},{12,4},{14,6},{16,24},{18,... | collective-permute-start | bytes 1572872 | tf_op jit(solution)/shard_map/ppermute | solution.py:265
  71.0 15.6 %collective-permute-start.10 = (bf16[2048,128]{1,0:T(8,128)(2,1)S(1)}, bf16[2048,128]{1,0:T(8,128)(2,1)S(1)}, u32[]{:S(2)}, u32[]{:S(2)}) collective-permute-start(bf16[2048,128]{1,0:T(8,128)(2,1)S(1)} %collective-permute-done.6.refs_8_), channel_id=1, source_target_pairs={{0,4},{2,6},{4,0},{6,2},{8,12},{10,14},{12,8},{14,10},{16,20},{18,... | collective-permute-start | bytes 1572872 | tf_op jit(solution)/shard_map/ppermute | solution.py:265
  72.5 14.9 %collective-permute-start.9 = (bf16[2048,128]{1,0:T(8,128)(2,1)S(1)}, bf16[2048,128]{1,0:T(8,128)(2,1)S(1)}, u32[]{:S(2)}, u32[]{:S(2)}) collective-permute-start(bf16[2048,128]{1,0:T(8,128)(2,1)S(1)} %collective-permute-done.6.refs_8_), channel_id=1, source_target_pairs={{0,2},{2,0},{4,6},{6,4},{8,10},{10,8},{12,14},{14,12},{16,18},{18,... | collective-permute-start | bytes 1572872 | tf_op jit(solution)/shard_map/ppermute | solution.py:265
  74.0 24.6 %collective-permute-start.18 = (bf16[2048,128]{1,0:T(8,128)(2,1)S(1)}, bf16[2048,128]{1,0:T(8,128)(2,1)S(1)}, u32[]{:S(2)}, u32[]{:S(2)}) collective-permute-start(bf16[2048,128]{1,0:T(8,128)(2,1)S(1)} %collective-permute-done.8.refs_14_), channel_id=1, source_target_pairs={{0,2},{2,0},{4,6},{6,4},{8,10},{10,8},{12,14},{14,12},{16,18},{18,... | collective-permute-start | bytes 1572872 | tf_op jit(solution)/shard_map/ppermute | solution.py:265
  77.5 19.7 %collective-permute-start.16 = (bf16[2048,128]{1,0:T(8,128)(2,1)S(1)}, bf16[2048,128]{1,0:T(8,128)(2,1)S(1)}, u32[]{:S(2)}, u32[]{:S(2)}) collective-permute-start(bf16[2048,128]{1,0:T(8,128)(2,1)S(1)} %collective-permute-done.14.refs_5_), channel_id=1, source_target_pairs={{0,4},{2,6},{4,0},{6,2},{8,12},{10,14},{12,8},{14,10},{16,20},{18,... | collective-permute-start | bytes 1572872 | tf_op jit(solution)/shard_map/ppermute | solution.py:265
  87.4 23.4 %collective-permute-start.17 = (bf16[2048,128]{1,0:T(8,128)(2,1)S(1)}, bf16[2048,128]{1,0:T(8,128)(2,1)S(1)}, u32[]{:S(2)}, u32[]{:S(2)}) collective-permute-start(bf16[2048,128]{1,0:T(8,128)(2,1)S(1)} %collective-permute-done.9.refs_9_), channel_id=1, source_target_pairs={{0,4},{2,6},{4,0},{6,2},{8,12},{10,14},{12,8},{14,10},{16,20},{18,... | collective-permute-start | bytes 1572872 | tf_op jit(solution)/shard_map/ppermute | solution.py:265
  87.9 12.6 %collective-permute-start.13 = (bf16[8,128,128]{2,1,0:T(8,128)(2,1)S(1)}, bf16[8,128,128]{2,1,0:T(8,128)(2,1)S(1)}, u32[]{:S(2)}, u32[]{:S(2)}) collective-permute-start(bf16[8,128,128]{2,1,0:T(8,128)(2,1)S(1)} %get-tuple-element.125.refs_0_), channel_id=1, source_target_pairs={{0,16},{2,18},{4,20},{6,22},{8,24},{10,26},{12,28},{14,30},{16,0},... | collective-permute-start | bytes 786440 | tf_op jit(solution)/shard_map/ppermute | solution.py:265
  90.0 20.7 %collective-permute-start.12 = (bf16[8,128,128]{2,1,0:T(8,128)(2,1)S(1)}, bf16[8,128,128]{2,1,0:T(8,128)(2,1)S(1)}, u32[]{:S(2)}, u32[]{:S(2)}) collective-permute-start(bf16[8,128,128]{2,1,0:T(8,128)(2,1)S(1)} %get-tuple-element.125.refs_0_), channel_id=1, source_target_pairs={{0,4},{2,6},{4,0},{6,2},{8,12},{10,14},{12,8},{14,10},{16,20},{18,... | collective-permute-start | bytes 786440 | tf_op jit(solution)/shard_map/ppermute | solution.py:265
  97.2 13.6 %collective-permute-start.11 = (bf16[8,128,128]{2,1,0:T(8,128)(2,1)S(1)}, bf16[8,128,128]{2,1,0:T(8,128)(2,1)S(1)}, u32[]{:S(2)}, u32[]{:S(2)}) collective-permute-start(bf16[8,128,128]{2,1,0:T(8,128)(2,1)S(1)} %get-tuple-element.125.refs_0_), channel_id=1, source_target_pairs={{0,2},{2,0},{4,6},{6,4},{8,10},{10,8},{12,14},{14,12},{16,18},{18,... | collective-permute-start | bytes 786440 | tf_op jit(solution)/shard_map/ppermute | solution.py:265
  98.6 21.3 %collective-permute-start.20 = (bf16[8,128,128]{2,1,0:T(8,128)(2,1)S(1)}, bf16[8,128,128]{2,1,0:T(8,128)(2,1)S(1)}, u32[]{:S(2)}, u32[]{:S(2)}) collective-permute-start(bf16[8,128,128]{2,1,0:T(8,128)(2,1)S(1)} %get-tuple-element.125.refs_0_), channel_id=1, source_target_pairs={{0,8},{2,10},{4,12},{6,14},{8,0},{10,2},{12,4},{14,6},{16,24},{18,... | collective-permute-start | bytes 786440 | tf_op jit(solution)/shard_map/ppermute | solution.py:265
  110.8 9.1 %collective-permute-start.19 = (bf16[8,128,128]{2,1,0:T(8,128)(2,1)S(1)}, bf16[8,128,128]{2,1,0:T(8,128)(2,1)S(1)}, u32[]{:S(2)}, u32[]{:S(2)}) collective-permute-start(bf16[8,128,128]{2,1,0:T(8,128)(2,1)S(1)} %collective-permute-done.12.refs_2_), channel_id=1, source_target_pairs={{0,2},{2,0},{4,6},{6,4},{8,10},{10,8},{12,14},{14,12},{16,18},{18,... | collective-permute-start | bytes 786440 | tf_op jit(solution)/shard_map/ppermute | solution.py:265
  113.9 7.6 %collective-permute-start.21 = (bf16[8,128,128]{2,1,0:T(8,128)(2,1)S(1)}, bf16[8,128,128]{2,1,0:T(8,128)(2,1)S(1)}, u32[]{:S(2)}, u32[]{:S(2)}) collective-permute-start(bf16[8,128,128]{2,1,0:T(8,128)(2,1)S(1)} %collective-permute-done.13.refs_4_), channel_id=1, source_target_pairs={{0,2},{2,0},{4,6},{6,4},{8,10},{10,8},{12,14},{14,12},{16,18},{18,... | collective-permute-start | bytes 786440 | tf_op jit(solution)/shard_map/ppermute | solution.py:265
  121.5 28.0 %collective-permute-start.24 = (bf16[16,2048,128]{2,1,0:T(8,128)(2,1)}, bf16[16,2048,128]{2,1,0:T(8,128)(2,1)}, u32[]{:S(2)}, u32[]{:S(2)}) collective-permute-start(bf16[16,2048,128]{2,1,0:T(8,128)(2,1)} %shard_map.122), channel_id=1, source_target_pairs={{0,1},{1,0},{2,3},{3,2},{4,5},{5,4},{6,7},{7,6},{8,9},{9,8},{10,11... | collective-permute-start | bytes 25165832 | tf_op jit(solution)/shard_map/ppermute | solution.py:530
  121.5 9.1 %collective-permute-start.29 = (bf16[8,128,128]{2,1,0:T(8,128)(2,1)S(1)}, bf16[8,128,128]{2,1,0:T(8,128)(2,1)S(1)}, u32[]{:S(2)}, u32[]{:S(2)}) collective-permute-start(bf16[8,128,128]{2,1,0:T(8,128)(2,1)S(1)} %collective-permute-done.21.refs_5_), channel_id=1, source_target_pairs={{0,4},{2,6},{4,0},{6,2},{8,12},{10,14},{12,8},{14,10},{16,20},{18,... | collective-permute-start | bytes 786440 | tf_op jit(solution)/shard_map/ppermute | solution.py:265
  123.7 9.1 %collective-permute-start.25 = (bf16[8,128,128]{2,1,0:T(8,128)(2,1)S(1)}, bf16[8,128,128]{2,1,0:T(8,128)(2,1)S(1)}, u32[]{:S(2)}, u32[]{:S(2)}) collective-permute-start(bf16[8,128,128]{2,1,0:T(8,128)(2,1)S(1)} %collective-permute-done.11.refs_1_), channel_id=1, source_target_pairs={{0,8},{2,10},{4,12},{6,14},{8,0},{10,2},{12,4},{14,6},{16,24},{18,... | collective-permute-start | bytes 786440 | tf_op jit(solution)/shard_map/ppermute | solution.py:265
  124.1 13.7 %collective-permute-start.26 = (bf16[8,128,128]{2,1,0:T(8,128)(2,1)S(1)}, bf16[8,128,128]{2,1,0:T(8,128)(2,1)S(1)}, u32[]{:S(2)}, u32[]{:S(2)}) collective-permute-start(bf16[8,128,128]{2,1,0:T(8,128)(2,1)S(1)} %collective-permute-done.12.refs_2_), channel_id=1, source_target_pairs={{0,8},{2,10},{4,12},{6,14},{8,0},{10,2},{12,4},{14,6},{16,24},{18,... | collective-permute-start | bytes 786440 | tf_op jit(solution)/shard_map/ppermute | solution.py:265
  125.7 12.0 %collective-permute-start.28 = (bf16[8,128,128]{2,1,0:T(8,128)(2,1)S(1)}, bf16[8,128,128]{2,1,0:T(8,128)(2,1)S(1)}, u32[]{:S(2)}, u32[]{:S(2)}) collective-permute-start(bf16[8,128,128]{2,1,0:T(8,128)(2,1)S(1)} %collective-permute-done.23.refs_4_), channel_id=1, source_target_pairs={{0,4},{2,6},{4,0},{6,2},{8,12},{10,14},{12,8},{14,10},{16,20},{18,... | collective-permute-start | bytes 786440 | tf_op jit(solution)/shard_map/ppermute | solution.py:265
  130.6 7.6 %collective-permute-start.27 = (bf16[8,128,128]{2,1,0:T(8,128)(2,1)S(1)}, bf16[8,128,128]{2,1,0:T(8,128)(2,1)S(1)}, u32[]{:S(2)}, u32[]{:S(2)}) collective-permute-start(bf16[8,128,128]{2,1,0:T(8,128)(2,1)S(1)} %collective-permute-done.23.refs_4_), channel_id=1, source_target_pairs={{0,2},{2,0},{4,6},{6,4},{8,10},{10,8},{12,14},{14,12},{16,18},{18,... | collective-permute-start | bytes 786440 | tf_op jit(solution)/shard_map/ppermute | solution.py:265
  138.2 10.4 %collective-permute-start.30 = (bf16[8,128,128]{2,1,0:T(8,128)(2,1)S(1)}, bf16[8,128,128]{2,1,0:T(8,128)(2,1)S(1)}, u32[]{:S(2)}, u32[]{:S(2)}) collective-permute-start(bf16[8,128,128]{2,1,0:T(8,128)(2,1)S(1)} %collective-permute-done.25.refs_1_.refs_5_), channel_id=1, source_target_pairs={{0,4},{2,6},{4,0},{6,2},{8,12},{10,14},{12,8},{14,10},{16,20},{18,... | collective-permute-start | bytes 786440 | tf_op jit(solution)/shard_map/ppermute | solution.py:265
  139.8 39.7 %all-to-all-start.1 = ((bf16[8,272,128]{2,1,0:T(8,128)(2,1)}), bf16[8,272,128]{2,1,0:T(8,128)(2,1)S(1)}, u32[]{:S(2)}, u32[]{:S(2)}) async-start(bf16[8,272,128]{2,1,0:T(8,128)(2,1)} %get-tuple-element.81), calls=%async_computation.1 | async-start | bytes 1114112 | tf_op jit(solution)/shard_map/all_to_all | solution.py:552
  143.3 20.9 %collective-permute-start.31 = (bf16[8,128,128]{2,1,0:T(8,128)(2,1)S(1)}, bf16[8,128,128]{2,1,0:T(8,128)(2,1)S(1)}, u32[]{:S(2)}, u32[]{:S(2)}) collective-permute-start(bf16[8,128,128]{2,1,0:T(8,128)(2,1)S(1)} %collective-permute-done.28.refs_6_), channel_id=1, source_target_pairs={{0,2},{2,0},{4,6},{6,4},{8,10},{10,8},{12,14},{14,12},{16,18},{18,... | collective-permute-start | bytes 786440 | tf_op jit(solution)/shard_map/ppermute | solution.py:265
  (15 other events, 113.8 us)

commit v3 on v2

--- a/solution.py
+++ b/solution.py
@@ -35,7 +35,7 @@
 def mm(a, b, dims):
     (ca,), (cb,) = dims[0]
     if isinstance(a, tuple) and isinstance(b, tuple):
-        return dot(join([a[0], a[1]], ca), join([b[0], b[0]], cb), dims) + dot(a[0], b[1], dims)
+        return dot(join([a[0], a[1], a[0]], ca), join([b[0], b[0], b[1]], cb), dims)
     if isinstance(a, tuple):
         return dot(join([a[0], a[1]], ca), join([b, b], cb), dims)
     if isinstance(b, tuple):
@@ -133,7 +133,7 @@
     return jnp.where(causal, jnp.exp(jnp.where(causal, run_col - run_row, 0.0)), 0.0)
 
 
-def first_kernel(place_ref, slab_ref, maps_ref, aux_ref, ends_ref, inv_ref, low_ref):
+def first_kernel(chained, place_ref, slab_ref, maps_ref, aux_ref, ends_ref, inv_ref, low_ref):
     count = slab_ref.shape[0]
     width = slab_ref.shape[2]
     length = (slab_ref.shape[1] - PAD) // 4
@@ -194,7 +194,8 @@
     for c in range(1, count):
         trans = split(maps_ref[c, 0])
         state = mm(trans, split(state), NN) + maps_ref[c, 1]
-        total = mm(trans, split(total), NN)
+        if chained:
+            total = mm(trans, split(total), NN)
         r = count - 1 - c
         adjoint = mm(split(adjoint), split(maps_ref[r, 0]), NN) + maps_ref[r, 2]
     ends_ref[0] = state
@@ -464,7 +465,7 @@
 
     square = (width, width)
     maps, aux, ends = whole_call(
-        first_kernel,
+        partial(first_kernel, groups > 2),
         [((count, 3) + square, f32), ((count, 4, length, width), f32), ((4,) + square, f32)],
         [((count, length, length), f32), ((count, length, length), f32)],
         9e9,

time: 181 us -> 183 us (1.011)
  Pallas kernels: 58.4 us -> 65.2 us
  waiting for transfers between devices: 55.9 us -> 50.6 us
    pallas_call x1, Pallas kernels: 9.65 us -> 16.6 us  [shards(): whole_call(partial(first_kernel, groups > 2), [((count, 3) + square, f32)...]
    ppermute x30, waiting for transfers between devices: 47 us -> 41.7 us  [swap(): lax.ppermute(x, 'seq', [(i, i ^ mask) for i in range(lax.axis_size('seq'))])]
  transfers between devices with their start and end apart: 34 -> 34, of which waited for: 12 -> 9; matrix products, arithmetic and copies ran while one was open for 0% -> 0% of each run, Pallas kernels for 30% -> 33%
where the time goes in v3:
time: 183 us
  Pallas kernels  65.2 us (36%)
  starting transfers between devices  60.7 us (33%)
  waiting for transfers between devices  50.6 us (28%)
  local copies, waits for them, and re-layouts  4.98 us (3%)
    ppermute x30, waiting for transfers between devices, swap(): lax.ppermute(x, 'seq', [(i, i ^ mask) for i in range(lax.axis_size('seq'))])  41.7 us
    ppermute x30, starting transfers between devices, swap(): lax.ppermute(x, 'seq', [(i, i ^ mask) for i in range(lax.axis_size('seq'))])  39.3 us
    pallas_call x2, Pallas kernels, weight_grad(): pl.pallas_call(partial(weight_kernel, starts), grid_spec=pltpu.PrefetchSc...  29.4 us
    pallas_call x1, Pallas kernels, shards(): whole_call(partial(first_kernel, groups > 2), [((count, 3) + square, f32)...  16.6 us
    ppermute x1, starting transfers between devices, shards(): start = finish = lax.ppermute(ends[3], 'seq', up + down)  10.3 us
    all_to_all x1, waiting for transfers between devices, shards(): lax.all_to_all(slabs, 'seq', 0, 0, axis_index_groups=members, tiled=True)  8.91 us
    pallas_call x1, Pallas kernels, shards(): whole_call(second_kernel, [((count, length, width), bf16), ((count, 2 * l...  7.48 us
    pallas_call x4, Pallas kernels, arranged(): pl.pallas_call(kernel, in_specs=[pl.BlockSpec(memory_space=pltpu.SMEM)] +...  7.37 us
  transfers between devices with their start and end apart: 34, of which 9 were waited for; matrix products, arithmetic and copies ran while one was open for 0% of the time, Pallas kernels for 33%

profile of v3, /device:TPU:0, one launch (start us, length us, event | category | flops | bytes accessed | tf_op | source)
XLA Modules:
  0.0 182.6 jit_solution(7135001158634848709)
XLA Ops:
  0.6 3.2 %shard_map.118 = bf16[8,528,128]{2,1,0:T(8,128)(2,1)} custom-call(bf16[128,1024]{1,0:T(8,128)(2,1)} %q_ref.1, bf16[128,1024]{1,0:T(8,128)(2,1)} %k_ref.1, bf16[128,1024]{1,0:T(8,128)(2,1)} %v_ref.1, bf16[128,1024]{1,0:T(8,128)(2,1)} %g_ref.1, f32[8,128]{1,0:T(8,128)} %bitcast.19, f32[8,128]{1,0:T(8,128)} %bitcast.20), custom_call_target="tpu_custom_call" | custom-call | tf_op jit(solution)/shard_map/pallas_call | solution.py:106
  3.9 6.2 %all-to-all-start = ((bf16[8,528,128]{2,1,0:T(8,128)(2,1)}), bf16[8,528,128]{2,1,0:T(8,128)(2,1)S(1)}, u32[]{:S(2)}, u32[]{:S(2)}) async-start(bf16[8,528,128]{2,1,0:T(8,128)(2,1)} %shard_map.118), calls=%async_computation | async-start | bytes 2162688 | tf_op jit(solution)/shard_map/all_to_all | solution.py:462
  10.3 4.1 %collective-permute-start.4 = (bf16[2048,128]{1,0:T(8,128)(2,1)S(1)}, bf16[2048,128]{1,0:T(8,128)(2,1)}, u32[]{:S(2)}, u32[]{:S(2)}) collective-permute-start(bf16[2048,128]{1,0:T(8,128)(2,1)S(1)} %shard_map.120.refs_0_), channel_id=1, source_target_pairs={{0,24},{2,26},{4,28},{6,30},{8,16},{10,18},{12,20},{14,22},{16,8},... | collective-permute-start | bytes 1572872 | tf_op jit(solution)/shard_map/ppermute | solution.py:266
  14.4 1.5 collective-permute-start.2
  17.4 8.9 %all-to-all-done.slab_ref = bf16[8,528,128]{2,1,0:T(8,128)(2,1)S(1)} async-done(((bf16[8,528,128]{2,1,0:T(8,128)(2,1)}), bf16[8,528,128]{2,1,0:T(8,128)(2,1)S(1)}, u32[]{:S(2)}, u32[]{:S(2)}) %all-to-all-start) | async-done | bytes 1081376 | tf_op jit(solution)/shard_map/all_to_all | solution.py:462
  26.3 16.6 %shard_map.119 = (f32[8,3,128,128]{3,2,1,0:T(8,128)S(1)}, f32[8,4,128,128]{3,2,1,0:T(8,128)S(1)}, f32[4,128,128]{2,1,0:T(8,128)S(1)}) custom-call(s32[2]{0:T(128)S(1)} %pad_add_fusion.place_ref, bf16[8,528,128]{2,1,0:T(8,128)(2,1)S(1)} %all-to-all-done.slab_ref), custom_call_target="tpu_custom_call" | custom-call | flops 8999999488 | tf_op jit(solution)/shard_map/pallas_call | solution.py:467
  42.9 10.3 %collective-permute-start = (f32[128,128]{1,0:T(8,128)S(1)}, f32[128,128]{1,0:T(8,128)S(1)}, u32[]{:S(2)}, u32[]{:S(2)}) collective-permute-start(f32[128,128]{1,0:T(8,128)S(1)} %slice_bitcast_fusion), channel_id=1, source_target_pairs={{0,16},{2,18},{4,20},{6,22},{8,24},{10,26},{12,28},{14,30},{16,0},... | collective-permute-start | bytes 196616 | tf_op jit(solution)/shard_map/ppermute | solution.py:485
  53.3 2.1 %collective-permute-start.5 = (bf16[2048,128]{1,0:T(8,128)(2,1)S(1)}, bf16[2048,128]{1,0:T(8,128)(2,1)S(1)}, u32[]{:S(2)}, u32[]{:S(2)}) collective-permute-start(bf16[2048,128]{1,0:T(8,128)(2,1)S(1)} %collective-permute-done.1.refs_1_), channel_id=1, source_target_pairs={{0,4},{2,6},{4,0},{6,2},{8,12},{10,14},{12,8},{14,10},{16,20},{18,... | collective-permute-start | bytes 1572872 | tf_op jit(solution)/shard_map/ppermute | solution.py:266
  55.5 1.9 %collective-permute-start.7 = (bf16[2048,128]{1,0:T(8,128)(2,1)}, bf16[2048,128]{1,0:T(8,128)(2,1)S(1)}, u32[]{:S(2)}, u32[]{:S(2)}) collective-permute-start(bf16[2048,128]{1,0:T(8,128)(2,1)} %collective-permute-done.4.refs_12_), channel_id=1, source_target_pairs={{0,2},{2,0},{4,6},{6,4},{8,10},{10,8},{12,14},{14,12},{16,18},{18,... | collective-permute-start | bytes 1572872 | tf_op jit(solution)/shard_map/ppermute | solution.py:266
  57.4 2.7 %collective-permute-start.6 = (bf16[2048,128]{1,0:T(8,128)(2,1)}, bf16[2048,128]{1,0:T(8,128)(2,1)S(1)}, u32[]{:S(2)}, u32[]{:S(2)}) collective-permute-start(bf16[2048,128]{1,0:T(8,128)(2,1)} %collective-permute-done.4.refs_12_), channel_id=1, source_target_pairs={{0,8},{2,10},{4,12},{6,14},{8,0},{10,2},{12,4},{14,6},{16,24},{18,... | collective-permute-start | bytes 1572872 | tf_op jit(solution)/shard_map/ppermute | solution.py:266
  60.2 5.2 %collective-permute-done.5.refs_3_ = bf16[2048,128]{1,0:T(8,128)(2,1)S(1)} collective-permute-done((bf16[2048,128]{1,0:T(8,128)(2,1)S(1)}, bf16[2048,128]{1,0:T(8,128)(2,1)S(1)}, u32[]{:S(2)}, u32[]{:S(2)}) %collective-permute-start.5) | collective-permute-done | bytes 524320 | tf_op jit(solution)/shard_map/ppermute | solution.py:266
  65.4 3.0 %collective-permute-start.15 = (bf16[2048,128]{1,0:T(8,128)(2,1)S(1)}, bf16[2048,128]{1,0:T(8,128)(2,1)S(1)}, u32[]{:S(2)}, u32[]{:S(2)}) collective-permute-start(bf16[2048,128]{1,0:T(8,128)(2,1)S(1)} %collective-permute-done.2.refs_2_), channel_id=1, source_target_pairs={{0,8},{2,10},{4,12},{6,14},{8,0},{10,2},{12,4},{14,6},{16,24},{18,... | collective-permute-start | bytes 1572872 | tf_op jit(solution)/shard_map/ppermute | solution.py:266
  68.4 8.3 %collective-permute-done.8.refs_14_ = bf16[2048,128]{1,0:T(8,128)(2,1)S(1)} collective-permute-done((bf16[2048,128]{1,0:T(8,128)(2,1)}, bf16[2048,128]{1,0:T(8,128)(2,1)S(1)}, u32[]{:S(2)}, u32[]{:S(2)}) %collective-permute-start.8) | collective-permute-done | bytes 524320 | tf_op jit(solution)/shard_map/ppermute | solution.py:266
  76.6 2.1 %collective-permute-start.10 = (bf16[2048,128]{1,0:T(8,128)(2,1)S(1)}, bf16[2048,128]{1,0:T(8,128)(2,1)S(1)}, u32[]{:S(2)}, u32[]{:S(2)}) collective-permute-start(bf16[2048,128]{1,0:T(8,128)(2,1)S(1)} %collective-permute-done.6.refs_8_), channel_id=1, source_target_pairs={{0,4},{2,6},{4,0},{6,2},{8,12},{10,14},{12,8},{14,10},{16,20},{18,... | collective-permute-start | bytes 1572872 | tf_op jit(solution)/shard_map/ppermute | solution.py:266
  78.7 1.5 collective-permute-start.9
  81.6 7.5 %shard_map.121 = (bf16[8,128,128]{2,1,0:T(8,128)(2,1)S(1)}, bf16[8,272,128]{2,1,0:T(8,128)(2,1)}) custom-call(s32[2]{0:T(128)S(1)} %pad_add_fusion.place_ref, bf16[8,528,128]{2,1,0:T(8,128)(2,1)S(1)} %all-to-all-done.slab_ref, f32[8,3,128,128]{3,2,1,0:T(8,128)S(1)} %get-tuple-element.74.maps_ref, f32[8,4,128,128]{3,2,1,0:T(8,128)S(1)} %get-tuple-element.75.aux_ref, ...), custom_call_target="tpu_custom_call" | custom-call | flops 7000000000 | tf_op jit(solution)/shard_map/pallas_call | solution.py:505
  89.1 2.5 %collective-permute-done.10.refs_10_ = bf16[2048,128]{1,0:T(8,128)(2,1)S(1)} collective-permute-done((bf16[2048,128]{1,0:T(8,128)(2,1)S(1)}, bf16[2048,128]{1,0:T(8,128)(2,1)S(1)}, u32[]{:S(2)}, u32[]{:S(2)}) %collective-permute-start.10) | collective-permute-done | bytes 524320 | tf_op jit(solution)/shard_map/ppermute | solution.py:266
  91.6 2.0 %collective-permute-start.17 = (bf16[2048,128]{1,0:T(8,128)(2,1)S(1)}, bf16[2048,128]{1,0:T(8,128)(2,1)S(1)}, u32[]{:S(2)}, u32[]{:S(2)}) collective-permute-start(bf16[2048,128]{1,0:T(8,128)(2,1)S(1)} %collective-permute-done.9.refs_9_), channel_id=1, source_target_pairs={{0,4},{2,6},{4,0},{6,2},{8,12},{10,14},{12,8},{14,10},{16,20},{18,... | collective-permute-start | bytes 1572872 | tf_op jit(solution)/shard_map/ppermute | solution.py:266
  93.6 1.6 collective-permute-start.12
  95.2 6.7 %collective-permute-done.16.refs_7_ = bf16[2048,128]{1,0:T(8,128)(2,1)S(1)} collective-permute-done((bf16[2048,128]{1,0:T(8,128)(2,1)S(1)}, bf16[2048,128]{1,0:T(8,128)(2,1)S(1)}, u32[]{:S(2)}, u32[]{:S(2)}) %collective-permute-start.16) | collective-permute-done | bytes 524320 | tf_op jit(solution)/shard_map/ppermute | solution.py:266
  103.8 9.3 %collective-permute-done.12.refs_2_ = bf16[8,128,128]{2,1,0:T(8,128)(2,1)S(1)} collective-permute-done((bf16[8,128,128]{2,1,0:T(8,128)(2,1)S(1)}, bf16[8,128,128]{2,1,0:T(8,128)(2,1)S(1)}, u32[]{:S(2)}, u32[]{:S(2)}) %collective-permute-start.12) | collective-permute-done | bytes 262176 | tf_op jit(solution)/shard_map/ppermute | solution.py:266
  113.1 1.5 collective-permute-start.19
  117.1 5.5 %shard_map.122 = bf16[16,2048,128]{2,1,0:T(8,128)(2,1)} custom-call(s32[1]{0:T(128)} %bitcast.6.me_ref, bf16[2048,128]{1,0:T(8,128)(2,1)S(1)} %shard_map.120.refs_0_, bf16[2048,128]{1,0:T(8,128)(2,1)S(1)} %collective-permute-done.1.refs_1_, bf16[2048,128]{1,0:T(8,128)(2,1)S(1)} %collective-permute-done.2.refs_2_, ...), custom_call_target="tpu_custom_call" | custom-call | tf_op jit(solution)/shard_map/pallas_call | solution.py:330
  124.5 1.8 collective-permute-start.25
  126.6 1.6 collective-permute-start.28
  128.2 4.3 %collective-permute-done.29.refs_7_ = bf16[8,128,128]{2,1,0:T(8,128)(2,1)S(1)} collective-permute-done((bf16[8,128,128]{2,1,0:T(8,128)(2,1)S(1)}, bf16[8,128,128]{2,1,0:T(8,128)(2,1)S(1)}, u32[]{:S(2)}, u32[]{:S(2)}) %collective-permute-start.29) | collective-permute-done | bytes 262176 | tf_op jit(solution)/shard_map/ppermute | solution.py:266
  134.7 3.9 %collective-permute-done.26.refs_2_.refs_6_ = bf16[8,128,128]{2,1,0:T(8,128)(2,1)S(1)} collective-permute-done((bf16[8,128,128]{2,1,0:T(8,128)(2,1)S(1)}, bf16[8,128,128]{2,1,0:T(8,128)(2,1)S(1)}, u32[]{:S(2)}, u32[]{:S(2)}) %collective-permute-start.26) | collective-permute-done | bytes 262176 | tf_op jit(solution)/shard_map/ppermute | solution.py:266
  138.6 1.5 collective-permute-done.27.refs_5_
  140.7 4.8 %all-to-all-start.1 = ((bf16[8,272,128]{2,1,0:T(8,128)(2,1)}), bf16[8,272,128]{2,1,0:T(8,128)(2,1)S(1)}, u32[]{:S(2)}, u32[]{:S(2)}) async-start(bf16[8,272,128]{2,1,0:T(8,128)(2,1)} %get-tuple-element.81), calls=%async_computation.1 | async-start | bytes 1114112 | tf_op jit(solution)/shard_map/all_to_all | solution.py:553
  145.5 2.0 %collective-permute-start.31 = (bf16[8,128,128]{2,1,0:T(8,128)(2,1)S(1)}, bf16[8,128,128]{2,1,0:T(8,128)(2,1)S(1)}, u32[]{:S(2)}, u32[]{:S(2)}) collective-permute-start(bf16[8,128,128]{2,1,0:T(8,128)(2,1)S(1)} %collective-permute-done.28.refs_6_), channel_id=1, source_target_pairs={{0,2},{2,0},{4,6},{6,4},{8,10},{10,8},{12,14},{14,12},{16,18},{18,... | collective-permute-start | bytes 786440 | tf_op jit(solution)/shard_map/ppermute | solution.py:266
  151.8 14.7 %shard_map.124.refs_3_ = bf16[4096,1024]{1,0:T(8,128)(2,1)} custom-call(s32[2]{0:T(128)S(1)} %pad_add_fusion.2.place_ref, bf16[16,1,2048,128]{3,2,1,0:T(8,128)(2,1)} %bitcast.17, bf16[16,1,2048,128]{3,2,1,0:T(8,128)(2,1)} %bitcast.8.refs_1_, bf16[2048,512]{1,0:T(8,128)(2,1)S(1)} %bitcast.15), custom_call_target="tpu_custom_call" | custom-call | flops 10000000000 | tf_op jit(solution)/shard_map/pallas_call | solution.py:404
  167.0 14.7 %shard_map.126 = bf16[4096,1024]{1,0:T(8,128)(2,1)} custom-call(s32[2]{0:T(128)S(1)} %pad_add_fusion.1.place_ref, bf16[16,1,2048,128]{3,2,1,0:T(8,128)(2,1)} %bitcast.18, bf16[16,1,2048,128]{3,2,1,0:T(8,128)(2,1)} %bitcast.8.refs_1_, bf16[2048,512]{1,0:T(8,128)(2,1)S(1)} %bitcast.16, ...), custom_call_target="tpu_custom_call", output_to_operand_aliasing={{}: (4, {})} | custom-call | flops 10000000000 | tf_op jit(solution)/shard_map/pallas_call | solution.py:404
  (77 shorter events, 18.2 us)
Async XLA Ops:
  3.9 22.4 %all-to-all-start = ((bf16[8,528,128]{2,1,0:T(8,128)(2,1)}), bf16[8,528,128]{2,1,0:T(8,128)(2,1)S(1)}, u32[]{:S(2)}, u32[]{:S(2)}) async-start(bf16[8,528,128]{2,1,0:T(8,128)(2,1)} %shard_map.118), calls=%async_computation | async-start | bytes 2162688 | tf_op jit(solution)/shard_map/all_to_all | solution.py:462
  10.3 43.0 %collective-permute-start.4 = (bf16[2048,128]{1,0:T(8,128)(2,1)S(1)}, bf16[2048,128]{1,0:T(8,128)(2,1)}, u32[]{:S(2)}, u32[]{:S(2)}) collective-permute-start(bf16[2048,128]{1,0:T(8,128)(2,1)S(1)} %shard_map.120.refs_0_), channel_id=1, source_target_pairs={{0,24},{2,26},{4,28},{6,30},{8,16},{10,18},{12,20},{14,22},{16,8},... | collective-permute-start | bytes 1572872 | tf_op jit(solution)/shard_map/ppermute | solution.py:266
  14.4 38.9 %collective-permute-start.3 = (bf16[2048,128]{1,0:T(8,128)(2,1)S(1)}, bf16[2048,128]{1,0:T(8,128)(2,1)S(1)}, u32[]{:S(2)}, u32[]{:S(2)}) collective-permute-start(bf16[2048,128]{1,0:T(8,128)(2,1)S(1)} %shard_map.120.refs_0_), channel_id=1, source_target_pairs={{0,8},{2,10},{4,12},{6,14},{8,0},{10,2},{12,4},{14,6},{16,24},{18,... | collective-permute-start | bytes 1572872 | tf_op jit(solution)/shard_map/ppermute | solution.py:266
  14.4 38.9 %collective-permute-start.2 = (bf16[2048,128]{1,0:T(8,128)(2,1)S(1)}, bf16[2048,128]{1,0:T(8,128)(2,1)S(1)}, u32[]{:S(2)}, u32[]{:S(2)}) collective-permute-start(bf16[2048,128]{1,0:T(8,128)(2,1)S(1)} %shard_map.120.refs_0_), channel_id=1, source_target_pairs={{0,4},{2,6},{4,0},{6,2},{8,12},{10,14},{12,8},{14,10},{16,20},{18,... | collective-permute-start | bytes 1572872 | tf_op jit(solution)/shard_map/ppermute | solution.py:266
  15.8 37.4 %collective-permute-start.1 = (bf16[2048,128]{1,0:T(8,128)(2,1)S(1)}, bf16[2048,128]{1,0:T(8,128)(2,1)S(1)}, u32[]{:S(2)}, u32[]{:S(2)}) collective-permute-start(bf16[2048,128]{1,0:T(8,128)(2,1)S(1)} %shard_map.120.refs_0_), channel_id=1, source_target_pairs={{0,2},{2,0},{4,6},{6,4},{8,10},{10,8},{12,14},{14,12},{16,18},{18,... | collective-permute-start | bytes 1572872 | tf_op jit(solution)/shard_map/ppermute | solution.py:266
  42.9 17.2 %collective-permute-start = (f32[128,128]{1,0:T(8,128)S(1)}, f32[128,128]{1,0:T(8,128)S(1)}, u32[]{:S(2)}, u32[]{:S(2)}) collective-permute-start(f32[128,128]{1,0:T(8,128)S(1)} %slice_bitcast_fusion), channel_id=1, source_target_pairs={{0,16},{2,18},{4,20},{6,22},{8,24},{10,26},{12,28},{14,30},{16,0},... | collective-permute-start | bytes 196616 | tf_op jit(solution)/shard_map/ppermute | solution.py:485
  53.3 12.1 %collective-permute-start.5 = (bf16[2048,128]{1,0:T(8,128)(2,1)S(1)}, bf16[2048,128]{1,0:T(8,128)(2,1)S(1)}, u32[]{:S(2)}, u32[]{:S(2)}) collective-permute-start(bf16[2048,128]{1,0:T(8,128)(2,1)S(1)} %collective-permute-done.1.refs_1_), channel_id=1, source_target_pairs={{0,4},{2,6},{4,0},{6,2},{8,12},{10,14},{12,8},{14,10},{16,20},{18,... | collective-permute-start | bytes 1572872 | tf_op jit(solution)/shard_map/ppermute | solution.py:266
  55.4 21.2 %collective-permute-start.8 = (bf16[2048,128]{1,0:T(8,128)(2,1)}, bf16[2048,128]{1,0:T(8,128)(2,1)S(1)}, u32[]{:S(2)}, u32[]{:S(2)}) collective-permute-start(bf16[2048,128]{1,0:T(8,128)(2,1)} %collective-permute-done.4.refs_12_), channel_id=1, source_target_pairs={{0,4},{2,6},{4,0},{6,2},{8,12},{10,14},{12,8},{14,10},{16,20},{18,... | collective-permute-start | bytes 1572872 | tf_op jit(solution)/shard_map/ppermute | solution.py:266
  55.5 21.2 %collective-permute-start.7 = (bf16[2048,128]{1,0:T(8,128)(2,1)}, bf16[2048,128]{1,0:T(8,128)(2,1)S(1)}, u32[]{:S(2)}, u32[]{:S(2)}) collective-permute-start(bf16[2048,128]{1,0:T(8,128)(2,1)} %collective-permute-done.4.refs_12_), channel_id=1, source_target_pairs={{0,2},{2,0},{4,6},{6,4},{8,10},{10,8},{12,14},{14,12},{16,18},{18,... | collective-permute-start | bytes 1572872 | tf_op jit(solution)/shard_map/ppermute | solution.py:266
  57.4 19.2 %collective-permute-start.6 = (bf16[2048,128]{1,0:T(8,128)(2,1)}, bf16[2048,128]{1,0:T(8,128)(2,1)S(1)}, u32[]{:S(2)}, u32[]{:S(2)}) collective-permute-start(bf16[2048,128]{1,0:T(8,128)(2,1)} %collective-permute-done.4.refs_12_), channel_id=1, source_target_pairs={{0,8},{2,10},{4,12},{6,14},{8,0},{10,2},{12,4},{14,6},{16,24},{18,... | collective-permute-start | bytes 1572872 | tf_op jit(solution)/shard_map/ppermute | solution.py:266
  60.1 20.6 %collective-permute-start.14 = (bf16[2048,128]{1,0:T(8,128)(2,1)S(1)}, bf16[2048,128]{1,0:T(8,128)(2,1)S(1)}, u32[]{:S(2)}, u32[]{:S(2)}) collective-permute-start(bf16[2048,128]{1,0:T(8,128)(2,1)S(1)} %collective-permute-done.1.refs_1_), channel_id=1, source_target_pairs={{0,8},{2,10},{4,12},{6,14},{8,0},{10,2},{12,4},{14,6},{16,24},{18,... | collective-permute-start | bytes 1572872 | tf_op jit(solution)/shard_map/ppermute | solution.py:266
  65.4 28.2 %collective-permute-start.15 = (bf16[2048,128]{1,0:T(8,128)(2,1)S(1)}, bf16[2048,128]{1,0:T(8,128)(2,1)S(1)}, u32[]{:S(2)}, u32[]{:S(2)}) collective-permute-start(bf16[2048,128]{1,0:T(8,128)(2,1)S(1)} %collective-permute-done.2.refs_2_), channel_id=1, source_target_pairs={{0,8},{2,10},{4,12},{6,14},{8,0},{10,2},{12,4},{14,6},{16,24},{18,... | collective-permute-start | bytes 1572872 | tf_op jit(solution)/shard_map/ppermute | solution.py:266
  76.6 14.9 %collective-permute-start.10 = (bf16[2048,128]{1,0:T(8,128)(2,1)S(1)}, bf16[2048,128]{1,0:T(8,128)(2,1)S(1)}, u32[]{:S(2)}, u32[]{:S(2)}) collective-permute-start(bf16[2048,128]{1,0:T(8,128)(2,1)S(1)} %collective-permute-done.6.refs_8_), channel_id=1, source_target_pairs={{0,4},{2,6},{4,0},{6,2},{8,12},{10,14},{12,8},{14,10},{16,20},{18,... | collective-permute-start | bytes 1572872 | tf_op jit(solution)/shard_map/ppermute | solution.py:266
  78.7 12.8 %collective-permute-start.9 = (bf16[2048,128]{1,0:T(8,128)(2,1)S(1)}, bf16[2048,128]{1,0:T(8,128)(2,1)S(1)}, u32[]{:S(2)}, u32[]{:S(2)}) collective-permute-start(bf16[2048,128]{1,0:T(8,128)(2,1)S(1)} %collective-permute-done.6.refs_8_), channel_id=1, source_target_pairs={{0,2},{2,0},{4,6},{6,4},{8,10},{10,8},{12,14},{14,12},{16,18},{18,... | collective-permute-start | bytes 1572872 | tf_op jit(solution)/shard_map/ppermute | solution.py:266
  80.2 23.2 %collective-permute-start.18 = (bf16[2048,128]{1,0:T(8,128)(2,1)S(1)}, bf16[2048,128]{1,0:T(8,128)(2,1)S(1)}, u32[]{:S(2)}, u32[]{:S(2)}) collective-permute-start(bf16[2048,128]{1,0:T(8,128)(2,1)S(1)} %collective-permute-done.8.refs_14_), channel_id=1, source_target_pairs={{0,2},{2,0},{4,6},{6,4},{8,10},{10,8},{12,14},{14,12},{16,18},{18,... | collective-permute-start | bytes 1572872 | tf_op jit(solution)/shard_map/ppermute | solution.py:266
  80.8 21.1 %collective-permute-start.16 = (bf16[2048,128]{1,0:T(8,128)(2,1)S(1)}, bf16[2048,128]{1,0:T(8,128)(2,1)S(1)}, u32[]{:S(2)}, u32[]{:S(2)}) collective-permute-start(bf16[2048,128]{1,0:T(8,128)(2,1)S(1)} %collective-permute-done.14.refs_5_), channel_id=1, source_target_pairs={{0,4},{2,6},{4,0},{6,2},{8,12},{10,14},{12,8},{14,10},{16,20},{18,... | collective-permute-start | bytes 1572872 | tf_op jit(solution)/shard_map/ppermute | solution.py:266
  91.6 21.6 %collective-permute-start.17 = (bf16[2048,128]{1,0:T(8,128)(2,1)S(1)}, bf16[2048,128]{1,0:T(8,128)(2,1)S(1)}, u32[]{:S(2)}, u32[]{:S(2)}) collective-permute-start(bf16[2048,128]{1,0:T(8,128)(2,1)S(1)} %collective-permute-done.9.refs_9_), channel_id=1, source_target_pairs={{0,4},{2,6},{4,0},{6,2},{8,12},{10,14},{12,8},{14,10},{16,20},{18,... | collective-permute-start | bytes 1572872 | tf_op jit(solution)/shard_map/ppermute | solution.py:266
  93.6 10.2 %collective-permute-start.13 = (bf16[8,128,128]{2,1,0:T(8,128)(2,1)S(1)}, bf16[8,128,128]{2,1,0:T(8,128)(2,1)S(1)}, u32[]{:S(2)}, u32[]{:S(2)}) collective-permute-start(bf16[8,128,128]{2,1,0:T(8,128)(2,1)S(1)} %get-tuple-element.125.refs_0_), channel_id=1, source_target_pairs={{0,16},{2,18},{4,20},{6,22},{8,24},{10,26},{12,28},{14,30},{16,0},... | collective-permute-start | bytes 786440 | tf_op jit(solution)/shard_map/ppermute | solution.py:266
  93.6 19.5 %collective-permute-start.12 = (bf16[8,128,128]{2,1,0:T(8,128)(2,1)S(1)}, bf16[8,128,128]{2,1,0:T(8,128)(2,1)S(1)}, u32[]{:S(2)}, u32[]{:S(2)}) collective-permute-start(bf16[8,128,128]{2,1,0:T(8,128)(2,1)S(1)} %get-tuple-element.125.refs_0_), channel_id=1, source_target_pairs={{0,4},{2,6},{4,0},{6,2},{8,12},{10,14},{12,8},{14,10},{16,20},{18,... | collective-permute-start | bytes 786440 | tf_op jit(solution)/shard_map/ppermute | solution.py:266
  101.9 11.2 %collective-permute-start.11 = (bf16[8,128,128]{2,1,0:T(8,128)(2,1)S(1)}, bf16[8,128,128]{2,1,0:T(8,128)(2,1)S(1)}, u32[]{:S(2)}, u32[]{:S(2)}) collective-permute-start(bf16[8,128,128]{2,1,0:T(8,128)(2,1)S(1)} %get-tuple-element.125.refs_0_), channel_id=1, source_target_pairs={{0,2},{2,0},{4,6},{6,4},{8,10},{10,8},{12,14},{14,12},{16,18},{18,... | collective-permute-start | bytes 786440 | tf_op jit(solution)/shard_map/ppermute | solution.py:266
  103.3 19.4 %collective-permute-start.20 = (bf16[8,128,128]{2,1,0:T(8,128)(2,1)S(1)}, bf16[8,128,128]{2,1,0:T(8,128)(2,1)S(1)}, u32[]{:S(2)}, u32[]{:S(2)}) collective-permute-start(bf16[8,128,128]{2,1,0:T(8,128)(2,1)S(1)} %get-tuple-element.125.refs_0_), channel_id=1, source_target_pairs={{0,8},{2,10},{4,12},{6,14},{8,0},{10,2},{12,4},{14,6},{16,24},{18,... | collective-permute-start | bytes 786440 | tf_op jit(solution)/shard_map/ppermute | solution.py:266
  113.1 9.6 %collective-permute-start.19 = (bf16[8,128,128]{2,1,0:T(8,128)(2,1)S(1)}, bf16[8,128,128]{2,1,0:T(8,128)(2,1)S(1)}, u32[]{:S(2)}, u32[]{:S(2)}) collective-permute-start(bf16[8,128,128]{2,1,0:T(8,128)(2,1)S(1)} %collective-permute-done.12.refs_2_), channel_id=1, source_target_pairs={{0,2},{2,0},{4,6},{6,4},{8,10},{10,8},{12,14},{14,12},{16,18},{18,... | collective-permute-start | bytes 786440 | tf_op jit(solution)/shard_map/ppermute | solution.py:266
  114.7 8.1 %collective-permute-start.23 = (bf16[8,128,128]{2,1,0:T(8,128)(2,1)S(1)}, bf16[8,128,128]{2,1,0:T(8,128)(2,1)S(1)}, u32[]{:S(2)}, u32[]{:S(2)}) collective-permute-start(bf16[8,128,128]{2,1,0:T(8,128)(2,1)S(1)} %collective-permute-done.13.refs_4_), channel_id=1, source_target_pairs={{0,8},{2,10},{4,12},{6,14},{8,0},{10,2},{12,4},{14,6},{16,24},{18,... | collective-permute-start | bytes 786440 | tf_op jit(solution)/shard_map/ppermute | solution.py:266
  115.1 7.6 %collective-permute-start.22 = (bf16[8,128,128]{2,1,0:T(8,128)(2,1)S(1)}, bf16[8,128,128]{2,1,0:T(8,128)(2,1)S(1)}, u32[]{:S(2)}, u32[]{:S(2)}) collective-permute-start(bf16[8,128,128]{2,1,0:T(8,128)(2,1)S(1)} %collective-permute-done.13.refs_4_), channel_id=1, source_target_pairs={{0,4},{2,6},{4,0},{6,2},{8,12},{10,14},{12,8},{14,10},{16,20},{18,... | collective-permute-start | bytes 786440 | tf_op jit(solution)/shard_map/ppermute | solution.py:266
  123.5 28.3 %collective-permute-start.24 = (bf16[16,2048,128]{2,1,0:T(8,128)(2,1)}, bf16[16,2048,128]{2,1,0:T(8,128)(2,1)}, u32[]{:S(2)}, u32[]{:S(2)}) collective-permute-start(bf16[16,2048,128]{2,1,0:T(8,128)(2,1)} %shard_map.122), channel_id=1, source_target_pairs={{0,1},{1,0},{2,3},{3,2},{4,5},{5,4},{6,7},{7,6},{8,9},{9,8},{10,11... | collective-permute-start | bytes 25165832 | tf_op jit(solution)/shard_map/ppermute | solution.py:531
  123.5 9.1 %collective-permute-start.29 = (bf16[8,128,128]{2,1,0:T(8,128)(2,1)S(1)}, bf16[8,128,128]{2,1,0:T(8,128)(2,1)S(1)}, u32[]{:S(2)}, u32[]{:S(2)}) collective-permute-start(bf16[8,128,128]{2,1,0:T(8,128)(2,1)S(1)} %collective-permute-done.21.refs_5_), channel_id=1, source_target_pairs={{0,4},{2,6},{4,0},{6,2},{8,12},{10,14},{12,8},{14,10},{16,20},{18,... | collective-permute-start | bytes 786440 | tf_op jit(solution)/shard_map/ppermute | solution.py:266
  124.5 10.2 %collective-permute-start.25 = (bf16[8,128,128]{2,1,0:T(8,128)(2,1)S(1)}, bf16[8,128,128]{2,1,0:T(8,128)(2,1)S(1)}, u32[]{:S(2)}, u32[]{:S(2)}) collective-permute-start(bf16[8,128,128]{2,1,0:T(8,128)(2,1)S(1)} %collective-permute-done.11.refs_1_), channel_id=1, source_target_pairs={{0,8},{2,10},{4,12},{6,14},{8,0},{10,2},{12,4},{14,6},{16,24},{18,... | collective-permute-start | bytes 786440 | tf_op jit(solution)/shard_map/ppermute | solution.py:266
  126.3 12.3 %collective-permute-start.26 = (bf16[8,128,128]{2,1,0:T(8,128)(2,1)S(1)}, bf16[8,128,128]{2,1,0:T(8,128)(2,1)S(1)}, u32[]{:S(2)}, u32[]{:S(2)}) collective-permute-start(bf16[8,128,128]{2,1,0:T(8,128)(2,1)S(1)} %collective-permute-done.12.refs_2_), channel_id=1, source_target_pairs={{0,8},{2,10},{4,12},{6,14},{8,0},{10,2},{12,4},{14,6},{16,24},{18,... | collective-permute-start | bytes 786440 | tf_op jit(solution)/shard_map/ppermute | solution.py:266
  126.6 12.0 %collective-permute-start.28 = (bf16[8,128,128]{2,1,0:T(8,128)(2,1)S(1)}, bf16[8,128,128]{2,1,0:T(8,128)(2,1)S(1)}, u32[]{:S(2)}, u32[]{:S(2)}) collective-permute-start(bf16[8,128,128]{2,1,0:T(8,128)(2,1)S(1)} %collective-permute-done.23.refs_4_), channel_id=1, source_target_pairs={{0,4},{2,6},{4,0},{6,2},{8,12},{10,14},{12,8},{14,10},{16,20},{18,... | collective-permute-start | bytes 786440 | tf_op jit(solution)/shard_map/ppermute | solution.py:266
  140.1 10.7 %collective-permute-start.30 = (bf16[8,128,128]{2,1,0:T(8,128)(2,1)S(1)}, bf16[8,128,128]{2,1,0:T(8,128)(2,1)S(1)}, u32[]{:S(2)}, u32[]{:S(2)}) collective-permute-start(bf16[8,128,128]{2,1,0:T(8,128)(2,1)S(1)} %collective-permute-done.25.refs_1_.refs_5_), channel_id=1, source_target_pairs={{0,4},{2,6},{4,0},{6,2},{8,12},{10,14},{12,8},{14,10},{16,20},{18,... | collective-permute-start | bytes 786440 | tf_op jit(solution)/shard_map/ppermute | solution.py:266
  140.7 41.0 %all-to-all-start.1 = ((bf16[8,272,128]{2,1,0:T(8,128)(2,1)}), bf16[8,272,128]{2,1,0:T(8,128)(2,1)S(1)}, u32[]{:S(2)}, u32[]{:S(2)}) async-start(bf16[8,272,128]{2,1,0:T(8,128)(2,1)} %get-tuple-element.81), calls=%async_computation.1 | async-start | bytes 1114112 | tf_op jit(solution)/shard_map/all_to_all | solution.py:553
  145.5 21.0 %collective-permute-start.31 = (bf16[8,128,128]{2,1,0:T(8,128)(2,1)S(1)}, bf16[8,128,128]{2,1,0:T(8,128)(2,1)S(1)}, u32[]{:S(2)}, u32[]{:S(2)}) collective-permute-start(bf16[8,128,128]{2,1,0:T(8,128)(2,1)S(1)} %collective-permute-done.28.refs_6_), channel_id=1, source_target_pairs={{0,2},{2,0},{4,6},{6,4},{8,10},{10,8},{12,14},{14,12},{16,18},{18,... | collective-permute-start | bytes 786440 | tf_op jit(solution)/shard_map/ppermute | solution.py:266
  (15 other events, 105.2 us)
